TPU v7x, 32 devices: a whole 2x2x4 slice. The times are simulated.
32 devices in a mesh: member: 4 (over z), region: 8 (over y, x, core).
Axes of the slice: x: 2, y: 2, z: 4, core: 2. Of those that a mesh axis runs over, the one named last changes fastest.
Arguments:
- ensemble: bfloat16 [256, 256, 512], P(('member', 'region')), may hold values from -6 to 6
- obs_site: int32 [256, 2048], P(('member', 'region')), may hold values from 0 to 511
- obs_blocks: int32 [256], P(('member', 'region')), may hold values from 1 to 16
- obs_precision: bfloat16 [256, 2048], P(('member', 'region')), may hold values from 0.049804688 to 1
- obs_innovation: bfloat16 [256, 2048], P(('member', 'region')), may hold values from -6 to 6
Outputs:
- analysis: bfloat16 [256, 256, 512], P(('member', 'region'))
Inputs may be any that keep to these rules, and one draw needn't show every extreme that they name: Only the first obs_blocks[p] blocks of 128 observations of patch p are used.
All inputs are finite; a program needn't handle non-finite values.
Results may differ from a plain program's by a relative error of at most 0.0062.
Values may be sent and summed in bfloat16 or wider, within the bound.
No kernel may reach another device: no remote copies, remote signals or barrier semaphores. Data moves between devices by JAX's collectives and lax.ppermute only.
A program may use at most 64 MiB of HBM per device.

v0:
```python
import jax
import jax.numpy as jnp
from jax import lax
from jax.sharding import PartitionSpec as P

OB = 128
ITERS = 6


def matmul_high(left, right):
    return jnp.matmul(left, right, precision=lax.Precision.HIGHEST)


def transform_weights(gram, rhs):
    members = gram.shape[-1]
    eye = jnp.eye(members, dtype=jnp.float32)
    amat = (members - 1.0) * eye + gram
    scale = jnp.sqrt(jnp.sum(amat * amat, axis=(-2, -1)))[..., None, None]
    yk = amat / scale
    zk = jnp.broadcast_to(eye, amat.shape)
    for step in range(ITERS):
        tk = 1.5 * eye - 0.5 * matmul_high(zk, yk)
        yk = matmul_high(yk, tk)
        zk = matmul_high(tk, zk)
    wmean = matmul_high(zk, matmul_high(zk, rhs[..., None]))[..., 0] / scale[..., 0]
    coef = wmean[..., :, None] + jnp.sqrt(members - 1.0) * zk / jnp.sqrt(scale)
    return coef.astype(jnp.bfloat16)


def block_sums(pert_one, sites_one, precision_one, innovation_one, blocks, first, stride):
    members = pert_one.shape[0]
    turns = (blocks - first + stride - 1) // stride

    def add_block(index, carry):
        gram, rhs = carry
        start = (first + index * stride) * OB
        picks = lax.dynamic_slice_in_dim(sites_one, start, OB)
        weight = lax.dynamic_slice_in_dim(precision_one, start, OB).astype(jnp.float32)
        values = lax.dynamic_slice_in_dim(innovation_one, start, OB)
        cols = jnp.take(pert_one, picks, axis=1)
        scaled = (cols.astype(jnp.float32) * weight[None, :]).astype(jnp.bfloat16)
        gram = gram + lax.dot_general(
            scaled, cols, (((1,), (1,)), ((), ())), preferred_element_type=jnp.float32
        )
        rhs = rhs + jnp.dot(scaled, values, preferred_element_type=jnp.float32)
        return (gram, rhs)

    start_sums = (jnp.zeros((members, members), jnp.float32), jnp.zeros((members,), jnp.float32))
    return lax.fori_loop(0, turns, add_block, start_sums)


def all_sums(pert, sites, precision, innovation, blocks, first, stride):
    grams = []
    sides = []
    for patch in range(pert.shape[1]):
        gram, rhs = block_sums(
            pert[:, patch, :],
            sites[patch],
            precision[patch],
            innovation[patch],
            blocks[patch],
            first,
            stride,
        )
        grams.append(gram)
        sides.append(rhs)
    return (jnp.stack(grams), jnp.stack(sides))


def local(ensemble, obs_site, obs_blocks, obs_precision, obs_innovation):
    gathered = lax.all_to_all(
        ensemble, ("member", "region"), split_axis=1, concat_axis=0, tiled=True
    )
    values = gathered.astype(jnp.float32)
    mean = jnp.mean(values, axis=0)
    pert = (values - mean[None]).astype(jnp.bfloat16)
    gram, rhs = all_sums(pert, obs_site, obs_precision, obs_innovation, obs_blocks, 0, 1)
    coef = transform_weights(gram, rhs)
    update = jnp.einsum("pjk,jps->kps", coef, pert, preferred_element_type=jnp.float32)
    analysed = (mean[None] + update).astype(jnp.bfloat16)
    return lax.all_to_all(analysed, ("member", "region"), split_axis=0, concat_axis=1, tiled=True)


def solution(mesh):
    placed = (
        P(("member", "region"), None, None),
        P(("member", "region"), None),
        P(("member", "region")),
        P(("member", "region"), None),
        P(("member", "region"), None),
    )
    return jax.shard_map(
        local,
        mesh=mesh,
        in_specs=placed,
        out_specs=P(("member", "region"), None, None),
        check_vma=False,
    )
```

profile of v0, /device:TPU:0, one launch (start us, length us, event | category | flops | bytes accessed | tf_op | source)
XLA Modules:
  0.0 544.4 jit_solution(7019405566441818773)
XLA Ops:
  0.0 4.1 copy.44
  4.1 7.3 %all-to-all-start = ((bf16[8,256,512]{2,0,1:T(8,128)(2,1)}), bf16[8,256,512]{2,0,1:T(8,128)(2,1)S(1)}, u32[]{:S(2)}, u32[]{:S(2)}) async-start(bf16[8,256,512]{2,0,1:T(8,128)(2,1)} %copy.44), calls=%async_computation | async-start | bytes 4194304 | tf_op jit(solution)/shard_map/all_to_all | solution.py:71
  15.2 45.0 %all-to-all-done = bf16[8,256,512]{2,0,1:T(8,128)(2,1)S(1)} async-done(((bf16[8,256,512]{2,0,1:T(8,128)(2,1)}), bf16[8,256,512]{2,0,1:T(8,128)(2,1)S(1)}, u32[]{:S(2)}, u32[]{:S(2)}) %all-to-all-start) | async-done | bytes 2097184 | tf_op jit(solution)/shard_map/all_to_all | solution.py:71
  62.8 4.5 fusion.137
  67.9 22.9 %while.96 = (s32[]{:T(128)}, f32[256,256]{1,0:T(8,128)S(1)}, f32[256]{0:T(256)S(1)}, s32[]{:T(128)}, s32[2048]{0:T(1024)S(1)}, /*index=5*/bf16[256,512]{0,1:T(8,...) while((s32[]{:T(128)}, f32[256,256]{1,0:T(8,128)S(1)}, ...), condition=%wide.region_3.5_spmd, body=%wide.region_2.4_spmd.sunk | while | flops 17205380 | bytes 799919 | solution.py:49
  92.0 14.0 %while.97 = (s32[]{:T(128)}, f32[256,256]{1,0:T(8,128)S(1)}, f32[256]{0:T(256)S(1)}, s32[]{:T(128)}, s32[2048]{0:T(1024)S(1)}, /*index=5*/bf16[256,512]{0,1:T(8,...) while((s32[]{:T(128)}, f32[256,256]{1,0:T(8,128)S(1)}, ...), condition=%wide.region_5.7_spmd, body=%wide.region_4.6_spmd.sunk | while | flops 17205380 | bytes 799919 | solution.py:49
  107.3 29.1 %while.98 = (s32[]{:T(128)}, f32[256,256]{1,0:T(8,128)S(1)}, f32[256]{0:T(256)S(1)}, s32[]{:T(128)}, s32[2048]{0:T(1024)S(1)}, /*index=5*/bf16[256,512]{0,1:T(8,...) while((s32[]{:T(128)}, f32[256,256]{1,0:T(8,128)S(1)}, ...), condition=%wide.region_7.9_spmd, body=%wide.region_6.8_spmd.sunk | while | flops 17205380 | bytes 799535 | solution.py:49
  138.5 71.2 %while.99 = (s32[]{:T(128)}, f32[256,256]{1,0:T(8,128)}, f32[256]{0:T(256)S(1)}, s32[]{:T(128)}, s32[2048]{0:T(1024)}, /*index=5*/bf16[256,512]{0,1:T(8,128)(2,1...) while((s32[]{:T(128)}, f32[256,256]{1,0:T(8,128)}, ...), condition=%wide.region_9.11_spmd, body=%wide.region_8.10_spmd.sunk | while | flops 17205380 | bytes 799535 | solution.py:49
  211.0 7.7 %while.100 = (s32[]{:T(128)}, f32[256,256]{1,0:T(8,128)S(1)}, f32[256]{0:T(256)S(1)}, s32[]{:T(128)}, s32[2048]{0:T(1024)S(1)}, /*index=5*/bf16[256,512]{0,1:T(8...) while((s32[]{:T(128)}, f32[256,256]{1,0:T(8,128)S(1)}, ...), condition=%wide.region_11.13_spmd, body=%wide.region_10.12_spmd.sunk | while | flops 17205380 | bytes 799535 | solution.py:49
  220.8 62.8 %while.101 = (s32[]{:T(128)}, f32[256,256]{1,0:T(8,128)}, f32[256]{0:T(256)S(1)}, s32[]{:T(128)}, s32[2048]{0:T(1024)S(1)}, /*index=5*/bf16[256,512]{0,1:T(8,128...) while((s32[]{:T(128)}, f32[256,256]{1,0:T(8,128)}, ...), condition=%wide.region_13.15_spmd, body=%wide.region_12.14_spmd.sunk | while | flops 17205380 | bytes 799535 | solution.py:49
  284.8 40.3 %while.102 = (s32[]{:T(128)}, f32[256,256]{1,0:T(8,128)S(1)}, f32[256]{0:T(256)S(1)}, s32[]{:T(128)}, s32[2048]{0:T(1024)S(1)}, /*index=5*/bf16[256,512]{0,1:T(8...) while((s32[]{:T(128)}, f32[256,256]{1,0:T(8,128)S(1)}, ...), condition=%wide.region_15.17_spmd, body=%wide.region_14.16_spmd.sunk | while | flops 17205380 | bytes 799535 | solution.py:49
  327.1 8.1 %while.103 = (s32[]{:T(128)}, f32[256,256]{1,0:T(8,128)S(1)}, f32[256]{0:T(256)S(1)}, s32[]{:T(128)}, s32[2048]{0:T(1024)S(1)}, /*index=5*/bf16[256,512]{0,1:T(8...) while((s32[]{:T(128)}, f32[256,256]{1,0:T(8,128)S(1)}, ...), condition=%wide.region_17.19_spmd, body=%wide.region_16.18_spmd.sunk | while | flops 17205380 | bytes 799535 | solution.py:49
  340.4 2.4 fusion.77
  342.8 2.1 fusion.78
  344.9 2.2 fusion.140
  347.1 2.3 fusion.79
  349.4 2.5 fusion.80
  351.9 2.2 fusion.141
  354.1 2.3 fusion.81
  356.4 2.3 fusion.82
  358.7 2.2 fusion.142
  360.9 2.6 fusion.83
  363.5 2.3 fusion.84
  365.8 2.2 fusion.143
  367.9 2.3 fusion.85
  370.3 2.3 fusion.86
  372.6 2.4 fusion.144
  375.0 3.6 fusion.74
  378.6 3.6 fusion.123
  384.2 3.4 fusion.87
  387.5 3.4 copy.56
  390.9 151.5 %all_to_all.27 = bf16[256,8,512]{2,1,0:T(8,128)(2,1)S(1)} all-to-all(bf16[256,8,512]{2,1,0:T(8,128)(2,1)S(1)} %copy.56), channel_id=1, replica_groups=mesh['member'=4,'region'=8] {'member','region'}, dimensions={0} | all-to-all | bytes 4194304 | tf_op jit(solution)/shard_map/all_to_all | solution.py:81
  (519 shorter events, 235.0 us)
Async XLA Ops:
  4.1 7.3 %copy-start.12 = (s32[8]{0:T(128)S(1)}, s32[8]{0:T(128)}, u32[]{:S(2)}) copy-start(s32[8]{0:T(128)} %param.25) | copy-start | bytes 100
  4.1 9.5 %copy-start.9 = (bf16[8,2048]{1,0:T(8,128)(2,1)S(1)}, bf16[8,2048]{1,0:T(8,128)(2,1)}, u32[]{:S(2)}) copy-start(bf16[8,2048]{1,0:T(8,128)(2,1)} %param.27) | copy-start | bytes 98308
  4.1 9.5 %copy-start.10 = (bf16[8,2048]{1,0:T(8,128)(2,1)S(1)}, bf16[8,2048]{1,0:T(8,128)(2,1)}, u32[]{:S(2)}) copy-start(bf16[8,2048]{1,0:T(8,128)(2,1)} %param.26) | copy-start | bytes 98308
  4.1 10.5 %copy-start.11 = (s32[8,2048]{1,0:T(8,128)S(1)}, s32[8,2048]{1,0:T(8,128)}, u32[]{:S(2)}) copy-start(s32[8,2048]{1,0:T(8,128)} %param.24) | copy-start | bytes 196612
  4.1 56.2 %all-to-all-start = ((bf16[8,256,512]{2,0,1:T(8,128)(2,1)}), bf16[8,256,512]{2,0,1:T(8,128)(2,1)S(1)}, u32[]{:S(2)}, u32[]{:S(2)}) async-start(bf16[8,256,512]{2,0,1:T(8,128)(2,1)} %copy.44), calls=%async_computation | async-start | bytes 4194304 | tf_op jit(solution)/shard_map/all_to_all | solution.py:71
  136.4 2.1 copy-start.1
  218.7 2.1 copy-start.2
  325.2 0.7 copy-start.5
  335.2 2.1 copy-start.3
  335.2 2.1 copy-start.4
  335.3 2.2 copy-start.6
  335.3 2.2 copy-start.8
  337.4 1.0 copy-start.7
  378.6 3.6 copy-start
where the time goes:
time: 554 us; the launch traced here: 544 us
  matrix products  153 us (28%)
  blocking collectives  152 us (27%)
  local copies, waits for them, and re-layouts  84 us (15%)
  other arithmetic  54.8 us (10%)
  loops' own time  47.4 us (9%)
  waiting for transfers between devices  45 us (8%)
  starting transfers between devices  7.3 us (1%)
    all_to_all x1, blocking collectives, local(): lax.all_to_all(analysed, ('member', 'region'), split_axis=0, concat_axis=...  152 us
    dot_general x63, matrix products, add_block(): lax.dot_general(scaled, cols, (((1,), (1,)), ((), ())), preferred_element...  59 us
    gather x63, local copies, waits for them, and re-layouts, add_block(): cols = jnp.take(pert_one, picks, axis=1)  53.4 us
    another operation x8, loops' own time, block_sums(): return lax.fori_loop(0, turns, add_block, start_sums)  47.4 us
    dot_general x19, matrix products, matmul_high(): return jnp.matmul(left, right, precision=lax.Precision.HIGHEST)  45.6 us
    dot_general x63, matrix products, add_block(): rhs = rhs + jnp.dot(scaled, values, preferred_element_type=jnp.float32)  45.2 us
    all_to_all x1, waiting for transfers between devices, local(): lax.all_to_all(ensemble, ('member', 'region'), split_axis=1, concat_axis=...  45 us
    convert_element_type x63, other arithmetic, add_block(): lax.dynamic_slice_in_dim(precision_one, start, OB).astype(jnp.float32)  36.6 us
  transfers between devices with their start and end apart: 1, of which 1 were waited for; matrix products, arithmetic and copies ran while one was open for 1% of the time, Pallas kernels for 0%

commit v1 on v0

v1 whole, which is shorter than its diff:
```python
import functools
import math

import jax
import jax.numpy as jnp
from jax import lax
from jax.experimental import pallas as pl
from jax.experimental.pallas import tpu as pltpu
from jax.sharding import PartitionSpec as P

OB = 128
ITERS = 6
LANES = 128
VMEM = pl.BlockSpec(memory_space=pltpu.VMEM)
SMEM = pl.BlockSpec(memory_space=pltpu.SMEM)
F32 = jnp.float32
BF16 = jnp.bfloat16
PARAMS = pltpu.CompilerParams(vmem_limit_bytes=40 * 2**20)


def cost(flops, touched):
    return pl.CostEstimate(flops=flops, bytes_accessed=touched, transcendentals=0)


def dot(left, right):
    return lax.dot_general(left, right, (((1,), (0,)), ((), ())), preferred_element_type=F32)


def dot_rows(left, right):
    return lax.dot_general(left, right, (((1,), (1,)), ((), ())), preferred_element_type=F32)


def split(value):
    high = value.astype(BF16)
    return high, (value - high.astype(F32)).astype(BF16)


def dot_split(left, right):
    return dot(left[0], right[0]) + (dot(left[0], right[1]) + dot(left[1], right[0]))


def site_sums_kernel(states, blocks_ref, site_ref, precision_ref, innovation_ref, weight_ref, value_ref):
    patches, slots = site_ref.shape
    groups = states // LANES
    rows = lax.broadcasted_iota(jnp.int32, (groups, slots), 0)
    lanes = lax.broadcasted_iota(jnp.int32, (LANES, slots), 0)
    slot = lax.broadcasted_iota(jnp.int32, (1, slots), 1)
    for patch in range(patches):
        sites = site_ref[patch : patch + 1, :]
        alive = slot < blocks_ref[patch] * OB
        live = jnp.where(alive, precision_ref[patch : patch + 1, :].astype(F32), 0.0)
        value = live * innovation_ref[patch : patch + 1, :].astype(F32)
        high = value.astype(BF16).astype(F32)
        picked = rows == sites // LANES
        left = jnp.concatenate(
            [jnp.where(picked, part, 0.0) for part in (live, high, value - high)], axis=0
        ).astype(BF16)
        right = jnp.where(lanes == sites % LANES, 1.0, 0.0).astype(BF16)
        sums = dot_rows(left, right)
        for group in range(groups):
            columns = slice(group * LANES, (group + 1) * LANES)
            weight_ref[patch : patch + 1, columns] = sums[group : group + 1]
            value_ref[patch : patch + 1, columns] = (
                sums[groups + group : groups + group + 1]
                + sums[2 * groups + group : 2 * groups + group + 1]
            )


def analyse_kernel(first, senders, weight_ref, value_ref, *refs):
    ins, outs = refs[:senders], refs[senders:]
    patches, part, states = ins[0].shape
    members = senders * part
    grid_rows = lax.broadcasted_iota(jnp.int32, (members, members), 0)
    grid_columns = lax.broadcasted_iota(jnp.int32, (members, members), 1)
    eye = jnp.where(grid_rows == grid_columns, 1.0, 0.0)
    every = range(patches)

    means, perts, rests, scales, sides = [], [], [], [], []
    for patch in every:
        total = sum(jnp.sum(ref[patch].astype(F32), axis=0, keepdims=True) for ref in ins)
        mean = total / members
        pert = jnp.concatenate([(ref[patch].astype(F32) - mean).astype(BF16) for ref in ins], axis=0)
        weight = weight_ref[first + patch : first + patch + 1, :]
        value = value_ref[first + patch : first + patch + 1, :]
        scaled = split(pert.astype(F32) * weight)
        gram = dot_rows(scaled[0], pert) + dot_rows(scaled[1], pert)
        sides.append(
            dot_rows(jnp.concatenate([jnp.broadcast_to(part_, (8, states)) for part_ in split(value)], axis=0), pert)
        )
        amat = (members - 1.0) * eye + gram
        square = jnp.sum(jnp.sum(amat * amat, axis=1, keepdims=True), axis=0, keepdims=True)
        scale = lax.rsqrt(square)
        means.append(mean)
        perts.append(pert)
        scales.append(scale)
        rests.append(eye - amat * scale)

    zs = [eye + 0.5 * rest for rest in rests]
    for step in range(1, ITERS):
        parts = [split(rest) for rest in rests]
        squares = [dot_split(part_, part_) for part_ in parts]
        halves = [split(square) for square in squares]
        rests = [
            0.75 * square + 0.25 * dot_split(half, part_)
            for square, half, part_ in zip(squares, halves, parts)
        ]
        zs = [z + 0.5 * dot_split(split(rest), split(z)) for rest, z in zip(rests, zs)]

    for patch in every:
        z = split(zs[patch])
        row = sides[patch][0:1] + sides[patch][8:9]
        for _ in range(2):
            high, low = split(jnp.broadcast_to(row, (8, members)))
            row = (dot(high, z[0]) + (dot(high, z[1]) + dot(low, z[0])))[0:1]
        wmean = row * scales[patch]
        coef = wmean + (math.sqrt(members - 1.0) * lax.sqrt(scales[patch])) * zs[patch]
        update = dot(coef.astype(BF16), perts[patch])
        result = (means[patch] + update).astype(BF16)
        for sender, ref in enumerate(outs):
            ref[patch] = result[sender * part : (sender + 1) * part]


def pack_kernel(first, count, regions, place_ref, ensemble_ref, *outs):
    held = ensemble_ref.shape[1] // (len(outs) * regions)
    for k, out in enumerate(outs):
        def region(j, carry):
            owner = (place_ref[0] ^ k) * regions + (place_ref[1] ^ j)
            rows = pl.ds(pl.multiple_of(owner * held, held), held)
            block = ensemble_ref[:, rows, :].astype(F32)[:, first : first + count, :]
            out[j] = jnp.swapaxes(block, 0, 1).astype(BF16)
            return carry

        lax.fori_loop(0, regions, region, 0)


def turn_kernel(*refs, ins):
    sources, outs = refs[:ins], refs[ins:]
    members = sources[0].shape[2]
    for j, out in enumerate(outs):
        for patch in range(out.shape[0]):
            out[patch] = jnp.concatenate([source[j, patch] for source in sources], axis=0)


def unturn_kernel(*refs, ins):
    sources, outs = refs[:ins], refs[ins:]
    members = outs[0].shape[2]
    for j, source in enumerate(sources):
        for patch in range(source.shape[0]):
            for k, out in enumerate(outs):
                out[j, patch] = source[patch, k * members : (k + 1) * members, :]


def unpack_kernel(chunks, regions, partners, place_ref, *refs):
    sources, out = refs[:-1], refs[-1]
    held = out.shape[1] // (partners * regions)
    for k in range(partners):
        def region(j, carry):
            owner = (place_ref[0] ^ k) * regions + (place_ref[1] ^ j)
            rows = pl.ds(pl.multiple_of(owner * held, held), held)
            block = jnp.concatenate(
                [sources[chunk * partners + k][j].astype(F32) for chunk in range(chunks)], axis=0
            )
            out[:, rows, :] = jnp.swapaxes(block, 0, 1).astype(BF16)
            return carry

        lax.fori_loop(0, regions, region, 0)


def exchange(blocks, axis):
    size = len(blocks)
    return [blocks[0]] + [
        lax.ppermute(blocks[k], axis, [(i, i ^ k) for i in range(size)]) for k in range(1, size)
    ]


def local(partners, regions, ensemble, obs_site, obs_blocks, obs_precision, obs_innovation):
    members, patches, states = ensemble.shape
    held = obs_site.shape[0]
    chunks = 4
    count = held // chunks
    place = jnp.stack([lax.axis_index("member"), lax.axis_index("region")]).astype(jnp.int32)
    total = members * partners * regions
    sums = jax.ShapeDtypeStruct((held, states), F32)
    z_block = jax.ShapeDtypeStruct((regions, count, members, states), BF16)
    r_block = jax.ShapeDtypeStruct((count, partners * members, states), BF16)
    chunk_bytes = 2 * count * total * states

    packed = [
        pl.pallas_call(
            functools.partial(pack_kernel, chunk * count, count, regions),
            out_shape=[z_block] * partners,
            in_specs=[SMEM, VMEM],
            out_specs=[VMEM] * partners,
            compiler_params=PARAMS,
            cost_estimate=cost(0, 2 * chunk_bytes),
            name="pack",
        )(place, ensemble)
        for chunk in range(chunks)
    ]
    weight, value = pl.pallas_call(
        functools.partial(site_sums_kernel, states),
        out_shape=[sums, sums],
        in_specs=[SMEM, VMEM, VMEM, VMEM],
        out_specs=[VMEM, VMEM],
        compiler_params=PARAMS,
        cost_estimate=cost(2 * held * 16 * 2048 * 128, 8 * held * 2048),
        name="site_sums",
    )(obs_blocks, obs_site, obs_precision, obs_innovation)

    finished = []
    for chunk in range(chunks):
        arrived = exchange(packed[chunk], "member")
        turned = pl.pallas_call(
            functools.partial(turn_kernel, ins=partners),
            out_shape=[r_block] * regions,
            in_specs=[VMEM] * partners,
            out_specs=[VMEM] * regions,
            compiler_params=PARAMS,
            cost_estimate=cost(0, 2 * chunk_bytes),
            name="turn",
        )(*arrived)
        gathered = exchange(turned, "region")
        analysed = pl.pallas_call(
            functools.partial(analyse_kernel, chunk * count, regions),
            out_shape=[r_block] * regions,
            in_specs=[VMEM] * (2 + regions),
            out_specs=[VMEM] * regions,
            compiler_params=PARAMS,
            cost_estimate=cost(count * 51 * 2 * total**3, 2 * chunk_bytes),
            name="analyse",
        )(weight, value, *gathered)
        back = exchange(analysed, "region")
        unturned = pl.pallas_call(
            functools.partial(unturn_kernel, ins=regions),
            out_shape=[z_block] * partners,
            in_specs=[VMEM] * regions,
            out_specs=[VMEM] * partners,
            compiler_params=PARAMS,
            cost_estimate=cost(0, 2 * chunk_bytes),
            name="unturn",
        )(*back)
        finished += exchange(unturned, "member")
    return pl.pallas_call(
        functools.partial(unpack_kernel, chunks, regions, partners),
        out_shape=jax.ShapeDtypeStruct(ensemble.shape, BF16),
        in_specs=[SMEM] + [VMEM] * len(finished),
        out_specs=VMEM,
        compiler_params=PARAMS,
        cost_estimate=cost(0, 2 * chunk_bytes * chunks),
        name="unpack",
    )(place, *finished)


def solution(mesh):
    placed = (
        P(("member", "region"), None, None),
        P(("member", "region"), None),
        P(("member", "region")),
        P(("member", "region"), None),
        P(("member", "region"), None),
    )
    return jax.shard_map(
        functools.partial(local, mesh.shape["member"], mesh.shape["region"]),
        mesh=mesh,
        in_specs=placed,
        out_specs=P(("member", "region"), None, None),
        check_vma=False,
    )
```

time: 554 us -> 182 us (0.33); the launches traced: 544 us -> 182 us
  matrix products: 153 us -> 0 us
  blocking collectives: 152 us -> 0 us
  starting transfers between devices: 7.3 us -> 108 us
  local copies, waits for them, and re-layouts: 84 us -> 1.61 us
  other arithmetic: 54.8 us -> 0.07 us
  loops' own time: 47.4 us -> 0 us
  Pallas kernels: 0 us -> 33.1 us
  waiting for transfers between devices: 45 us -> 38.8 us
    dot_general x146 -> x0, matrix products: 153 us -> none  [the longest x63 59 us: add_block(): lax.dot_general(scaled, cols, (((1,), (1,)), ((), ())), preferred_element...]
    all_to_all x1 -> x0, blocking collectives: 152 us -> none  [local(): lax.all_to_all(analysed, ('member', 'region'), split_axis=0, concat_axis=...]
    ppermute x0 -> x80, starting transfers between devices: none -> 108 us  [exchange(): lax.ppermute(blocks[k], axis, [(i, i ^ k) for i in range(size)])]
    gather x63 -> x0, local copies, waits for them, and re-layouts: 53.4 us -> none  [add_block(): cols = jnp.take(pert_one, picks, axis=1)]
    another operation x8 -> x0, loops' own time: 47.4 us -> none  [block_sums(): return lax.fori_loop(0, turns, add_block, start_sums)]
    all_to_all x1 -> x0, waiting for transfers between devices: 45 us -> none  [local(): lax.all_to_all(ensemble, ('member', 'region'), split_axis=1, concat_axis=...]
    ppermute x0 -> x80, waiting for transfers between devices: none -> 38.8 us  [exchange(): lax.ppermute(blocks[k], axis, [(i, i ^ k) for i in range(size)])]
    convert_element_type x66 -> x0, other arithmetic: 38.6 us -> none  [the longest x63 36.6 us: add_block(): lax.dynamic_slice_in_dim(precision_one, start, OB).astype(jnp.float32)]
  transfers between devices with their start and end apart: 1 -> 80, of which waited for: 1 -> 16; matrix products, arithmetic and copies ran while one was open for 1% -> 0% of each run, Pallas kernels for 0% -> 16%
where the time goes in v1:
time: 182 us
  starting transfers between devices  108 us (59%)
  waiting for transfers between devices  38.8 us (21%)
  Pallas kernels  33.1 us (18%)
    ppermute x80, starting transfers between devices, exchange(): lax.ppermute(blocks[k], axis, [(i, i ^ k) for i in range(size)])  108 us
    ppermute x80, waiting for transfers between devices, exchange(): lax.ppermute(blocks[k], axis, [(i, i ^ k) for i in range(size)])  38.8 us
    pallas_call x4, Pallas kernels, local(): pl.pallas_call(functools.partial(analyse_kernel, chunk * count, regions),...  22.4 us
    pallas_call x4, Pallas kernels, local(): pl.pallas_call(functools.partial(pack_kernel, chunk * count, count, regio...  5.5 us
  transfers between devices with their start and end apart: 80, of which 16 were waited for; matrix products, arithmetic and copies ran while one was open for 0% of the time, Pallas kernels for 16%

profile of v1, /device:TPU:0, one launch (start us, length us, event | category | flops | bytes accessed | tf_op | source)
XLA Modules:
  0.0 181.6 jit_solution(5702926033114114404)
XLA Ops:
  3.0 3.1 %collective-permute-start.20 = (bf16[8,2,8,512]{3,2,1,0:T(8,128)(2,1)S(1)}, bf16[8,2,8,512]{3,2,1,0:T(8,128)(2,1)S(1)}, u32[]{:S(2)}, u32[]{:S(2)}) collective-permute-start(bf16[8,2,8,512]{3,2,1,0:T(8,128)(2,1)S(1)} %get-tuple-element.130), channel_id=1, source_target_pairs={{0,8},{8,0},{16,24},{24,16},{1,9},{9,1},{17,25},{25,17},{2,10},{10... | collective-permute-start | bytes 393224 | tf_op jit(solution)/shard_map/ppermute | solution.py:172
  6.1 2.6 %collective-permute-start.21 = (bf16[8,2,8,512]{3,2,1,0:T(8,128)(2,1)S(1)}, bf16[8,2,8,512]{3,2,1,0:T(8,128)(2,1)S(1)}, u32[]{:S(2)}, u32[]{:S(2)}) collective-permute-start(bf16[8,2,8,512]{3,2,1,0:T(8,128)(2,1)S(1)} %get-tuple-element.131), channel_id=1, source_target_pairs={{0,16},{8,24},{16,0},{24,8},{1,17},{9,25},{17,1},{25,9},{2,18},{10... | collective-permute-start | bytes 393224 | tf_op jit(solution)/shard_map/ppermute | solution.py:172
  11.1 3.5 %collective-permute-start.1 = (bf16[8,2,8,512]{3,2,1,0:T(8,128)(2,1)S(1)}, bf16[8,2,8,512]{3,2,1,0:T(8,128)(2,1)S(1)}, u32[]{:S(2)}, u32[]{:S(2)}) collective-permute-start(bf16[8,2,8,512]{3,2,1,0:T(8,128)(2,1)S(1)} %get-tuple-element.107), channel_id=1, source_target_pairs={{0,16},{8,24},{16,0},{24,8},{1,17},{9,25},{17,1},{25,9},{2,18},{10... | collective-permute-start | bytes 393224 | tf_op jit(solution)/shard_map/ppermute | solution.py:172
  16.0 3.1 %collective-permute-done.21.refs_2_ = bf16[8,2,8,512]{3,2,1,0:T(8,128)(2,1)S(1)} collective-permute-done((bf16[8,2,8,512]{3,2,1,0:T(8,128)(2,1)S(1)}, bf16[8,2,8,512]{3,2,1,0:T(8,128)(2,1)S(1)}, u32[]{:S(2)}, u32[]{:S(2)}) %collective-permute-start.21) | collective-permute-done | bytes 131104 | tf_op jit(solution)/shard_map/ppermute | solution.py:172
  20.6 9.0 %collective-permute-start.61 = (bf16[8,2,8,512]{3,2,1,0:T(8,128)(2,1)S(1)}, bf16[8,2,8,512]{3,2,1,0:T(8,128)(2,1)S(1)}, u32[]{:S(2)}, u32[]{:S(2)}) collective-permute-start(bf16[8,2,8,512]{3,2,1,0:T(8,128)(2,1)S(1)} %get-tuple-element.179), channel_id=1, source_target_pairs={{0,16},{8,24},{16,0},{24,8},{1,17},{9,25},{17,1},{25,9},{2,18},{10... | collective-permute-start | bytes 393224 | tf_op jit(solution)/shard_map/ppermute | solution.py:172
  30.4 4.0 %collective-permute-done.1.refs_2_ = bf16[8,2,8,512]{3,2,1,0:T(8,128)(2,1)S(1)} collective-permute-done((bf16[8,2,8,512]{3,2,1,0:T(8,128)(2,1)S(1)}, bf16[8,2,8,512]{3,2,1,0:T(8,128)(2,1)S(1)}, u32[]{:S(2)}, u32[]{:S(2)}) %collective-permute-start.1) | collective-permute-done | bytes 131104 | tf_op jit(solution)/shard_map/ppermute | solution.py:172
  35.3 4.9 %collective-permute-start.41 = (bf16[8,2,8,512]{3,2,1,0:T(8,128)(2,1)S(1)}, bf16[8,2,8,512]{3,2,1,0:T(8,128)(2,1)S(1)}, u32[]{:S(2)}, u32[]{:S(2)}) collective-permute-start(bf16[8,2,8,512]{3,2,1,0:T(8,128)(2,1)S(1)} %get-tuple-element.155), channel_id=1, source_target_pairs={{0,16},{8,24},{16,0},{24,8},{1,17},{9,25},{17,1},{25,9},{2,18},{10... | collective-permute-start | bytes 393224 | tf_op jit(solution)/shard_map/ppermute | solution.py:172
  41.8 5.4 %collective-permute-done.61.refs_2_ = bf16[8,2,8,512]{3,2,1,0:T(8,128)(2,1)S(1)} collective-permute-done((bf16[8,2,8,512]{3,2,1,0:T(8,128)(2,1)S(1)}, bf16[8,2,8,512]{3,2,1,0:T(8,128)(2,1)S(1)}, u32[]{:S(2)}, u32[]{:S(2)}) %collective-permute-start.61) | collective-permute-done | bytes 131104 | tf_op jit(solution)/shard_map/ppermute | solution.py:172
  49.1 3.7 %collective-permute-done.41.refs_2_ = bf16[8,2,8,512]{3,2,1,0:T(8,128)(2,1)S(1)} collective-permute-done((bf16[8,2,8,512]{3,2,1,0:T(8,128)(2,1)S(1)}, bf16[8,2,8,512]{3,2,1,0:T(8,128)(2,1)S(1)}, u32[]{:S(2)}, u32[]{:S(2)}) %collective-permute-start.41) | collective-permute-done | bytes 131104 | tf_op jit(solution)/shard_map/ppermute | solution.py:172
  60.0 3.6 %collective-permute-start.6 = (bf16[2,32,512]{2,1,0:T(8,128)(2,1)S(1)}, bf16[2,32,512]{2,1,0:T(8,128)(2,1)S(1)}, u32[]{:S(2)}, u32[]{:S(2)}) collective-permute-start(bf16[2,32,512]{2,1,0:T(8,128)(2,1)S(1)} %get-tuple-element.113), channel_id=1, source_target_pairs={{0,4},{1,5},{2,6},{3,7},{4,0},{5,1},{6,2},{7,3},{8,12},{9,13},{10,... | collective-permute-start | bytes 196616 | tf_op jit(solution)/shard_map/ppermute | solution.py:172
  67.5 2.6 %collective-permute-start.65 = (bf16[2,32,512]{2,1,0:T(8,128)(2,1)S(1)}, bf16[2,32,512]{2,1,0:T(8,128)(2,1)S(1)}, u32[]{:S(2)}, u32[]{:S(2)}) collective-permute-start(bf16[2,32,512]{2,1,0:T(8,128)(2,1)S(1)} %get-tuple-element.184), channel_id=1, source_target_pairs={{0,3},{1,2},{2,1},{3,0},{4,7},{5,6},{6,5},{7,4},{8,11},{9,10},{10,... | collective-permute-start | bytes 196616 | tf_op jit(solution)/shard_map/ppermute | solution.py:172
  70.2 1.9 %collective-permute-start.67 = (bf16[2,32,512]{2,1,0:T(8,128)(2,1)S(1)}, bf16[2,32,512]{2,1,0:T(8,128)(2,1)S(1)}, u32[]{:S(2)}, u32[]{:S(2)}) collective-permute-start(bf16[2,32,512]{2,1,0:T(8,128)(2,1)S(1)} %get-tuple-element.186), channel_id=1, source_target_pairs={{0,5},{1,4},{2,7},{3,6},{4,1},{5,0},{6,3},{7,2},{8,13},{9,12},{10,... | collective-permute-start | bytes 196616 | tf_op jit(solution)/shard_map/ppermute | solution.py:172
  76.5 1.7 site_sums.1
  80.5 2.1 %collective-permute-start.48 = (bf16[2,32,512]{2,1,0:T(8,128)(2,1)S(1)}, bf16[2,32,512]{2,1,0:T(8,128)(2,1)S(1)}, u32[]{:S(2)}, u32[]{:S(2)}) collective-permute-start(bf16[2,32,512]{2,1,0:T(8,128)(2,1)S(1)} %get-tuple-element.163), channel_id=1, source_target_pairs={{0,6},{1,7},{2,4},{3,5},{4,2},{5,3},{6,0},{7,1},{8,14},{9,15},{10,... | collective-permute-start | bytes 196616 | tf_op jit(solution)/shard_map/ppermute | solution.py:172
  82.8 5.6 %analyse.5 = (bf16[2,32,512]{2,1,0:T(8,128)(2,1)S(1)}, bf16[2,32,512]{2,1,0:T(8,128)(2,1)S(1)}, bf16[2,32,512]{2,1,0:T(8,128)(2,1)S(1)}, bf16[2,32,512]{2,1,0:T(...) custom-call(f32[8,512]{1,0:T(8,128)S(1)} %get-tuple-element.103.weig, ...), custom_call_target="tpu_custom_call" | custom-call | flops 3422552064 | bytes 1048576 | tf_op jit(solution)/shard_map/analyse/pallas_call | solution.py:223
  92.7 5.8 %analyse.4 = (bf16[2,32,512]{2,1,0:T(8,128)(2,1)S(1)}, bf16[2,32,512]{2,1,0:T(8,128)(2,1)S(1)}, bf16[2,32,512]{2,1,0:T(8,128)(2,1)S(1)}, bf16[2,32,512]{2,1,0:T(...) custom-call(f32[8,512]{1,0:T(8,128)S(1)} %get-tuple-element.103.weig, ...), custom_call_target="tpu_custom_call" | custom-call | flops 3422552064 | bytes 1048576 | tf_op jit(solution)/shard_map/analyse/pallas_call | solution.py:223
  98.4 2.1 %collective-permute-start.35 = (bf16[2,32,512]{2,1,0:T(8,128)(2,1)S(1)}, bf16[2,32,512]{2,1,0:T(8,128)(2,1)S(1)}, u32[]{:S(2)}, u32[]{:S(2)}) collective-permute-start(bf16[2,32,512]{2,1,0:T(8,128)(2,1)S(1)} %get-tuple-element.147), channel_id=1, source_target_pairs={{0,6},{1,7},{2,4},{3,5},{4,2},{5,3},{6,0},{7,1},{8,14},{9,15},{10,... | collective-permute-start | bytes 196616 | tf_op jit(solution)/shard_map/ppermute | solution.py:172
  103.0 5.6 %analyse.7 = (bf16[2,32,512]{2,1,0:T(8,128)(2,1)S(1)}, bf16[2,32,512]{2,1,0:T(8,128)(2,1)S(1)}, bf16[2,32,512]{2,1,0:T(8,128)(2,1)S(1)}, bf16[2,32,512]{2,1,0:T(...) custom-call(f32[8,512]{1,0:T(8,128)S(1)} %get-tuple-element.103.weig, ...), custom_call_target="tpu_custom_call" | custom-call | flops 3422552064 | bytes 1048576 | tf_op jit(solution)/shard_map/analyse/pallas_call | solution.py:223
  110.7 2.1 %collective-permute-start.15 = (bf16[2,32,512]{2,1,0:T(8,128)(2,1)S(1)}, bf16[2,32,512]{2,1,0:T(8,128)(2,1)S(1)}, u32[]{:S(2)}, u32[]{:S(2)}) collective-permute-start(bf16[2,32,512]{2,1,0:T(8,128)(2,1)S(1)} %get-tuple-element.123), channel_id=1, source_target_pairs={{0,6},{1,7},{2,4},{3,5},{4,2},{5,3},{6,0},{7,1},{8,14},{9,15},{10,... | collective-permute-start | bytes 196616 | tf_op jit(solution)/shard_map/ppermute | solution.py:172
  115.5 3.2 %collective-permute-start.72 = (bf16[2,32,512]{2,1,0:T(8,128)(2,1)S(1)}, bf16[2,32,512]{2,1,0:T(8,128)(2,1)S(1)}, u32[]{:S(2)}, u32[]{:S(2)}) collective-permute-start(bf16[2,32,512]{2,1,0:T(8,128)(2,1)S(1)} %get-tuple-element.192), channel_id=1, source_target_pairs={{0,3},{1,2},{2,1},{3,0},{4,7},{5,6},{6,5},{7,4},{8,11},{9,10},{10,... | collective-permute-start | bytes 196616 | tf_op jit(solution)/shard_map/ppermute | solution.py:172
  121.0 5.6 %analyse.6 = (bf16[2,32,512]{2,1,0:T(8,128)(2,1)S(1)}, bf16[2,32,512]{2,1,0:T(8,128)(2,1)S(1)}, bf16[2,32,512]{2,1,0:T(8,128)(2,1)S(1)}, bf16[2,32,512]{2,1,0:T(...) custom-call(f32[8,512]{1,0:T(8,128)S(1)} %get-tuple-element.103.weig, ...), custom_call_target="tpu_custom_call" | custom-call | flops 3422552064 | bytes 1048576 | tf_op jit(solution)/shard_map/analyse/pallas_call | solution.py:223
  126.6 2.1 %collective-permute-start.76 = (bf16[2,32,512]{2,1,0:T(8,128)(2,1)S(1)}, bf16[2,32,512]{2,1,0:T(8,128)(2,1)S(1)}, u32[]{:S(2)}, u32[]{:S(2)}) collective-permute-start(bf16[2,32,512]{2,1,0:T(8,128)(2,1)S(1)} %get-tuple-element.196), channel_id=1, source_target_pairs={{0,7},{1,6},{2,5},{3,4},{4,3},{5,2},{6,1},{7,0},{8,15},{9,14},{10,... | collective-permute-start | bytes 196616 | tf_op jit(solution)/shard_map/ppermute | solution.py:172
  131.9 2.9 %collective-permute-start.38 = (bf16[8,2,8,512]{3,2,1,0:T(8,128)(2,1)S(1)}, bf16[8,2,8,512]{3,2,1,0:T(8,128)(2,1)S(1)}, u32[]{:S(2)}, u32[]{:S(2)}) collective-permute-start(bf16[8,2,8,512]{3,2,1,0:T(8,128)(2,1)S(1)} %get-tuple-element.151), channel_id=1, source_target_pairs={{0,16},{8,24},{16,0},{24,8},{1,17},{9,25},{17,1},{25,9},{2,18},{10... | collective-permute-start | bytes 393224 | tf_op jit(solution)/shard_map/ppermute | solution.py:172
  134.8 2.6 %collective-permute-start.55 = (bf16[2,32,512]{2,1,0:T(8,128)(2,1)S(1)}, bf16[2,32,512]{2,1,0:T(8,128)(2,1)S(1)}, u32[]{:S(2)}, u32[]{:S(2)}) collective-permute-start(bf16[2,32,512]{2,1,0:T(8,128)(2,1)S(1)} %get-tuple-element.171), channel_id=1, source_target_pairs={{0,6},{1,7},{2,4},{3,5},{4,2},{5,3},{6,0},{7,1},{8,14},{9,15},{10,... | collective-permute-start | bytes 196616 | tf_op jit(solution)/shard_map/ppermute | solution.py:172
  143.3 1.7 collective-permute-start.19
  147.1 2.3 %collective-permute-start.78 = (bf16[8,2,8,512]{3,2,1,0:T(8,128)(2,1)S(1)}, bf16[8,2,8,512]{3,2,1,0:T(8,128)(2,1)S(1)}, u32[]{:S(2)}, u32[]{:S(2)}) collective-permute-start(bf16[8,2,8,512]{3,2,1,0:T(8,128)(2,1)S(1)} %get-tuple-element.199), channel_id=1, source_target_pairs={{0,16},{8,24},{16,0},{24,8},{1,17},{9,25},{17,1},{25,9},{2,18},{10... | collective-permute-start | bytes 393224 | tf_op jit(solution)/shard_map/ppermute | solution.py:172
  151.7 4.5 %collective-permute-done.18.refs_2_ = bf16[8,2,8,512]{3,2,1,0:T(8,128)(2,1)S(1)} collective-permute-done((bf16[8,2,8,512]{3,2,1,0:T(8,128)(2,1)S(1)}, bf16[8,2,8,512]{3,2,1,0:T(8,128)(2,1)S(1)}, u32[]{:S(2)}, u32[]{:S(2)}) %collective-permute-start.18) | collective-permute-done | bytes 131104 | tf_op jit(solution)/shard_map/ppermute | solution.py:172
  156.2 9.5 %collective-permute-start.58 = (bf16[8,2,8,512]{3,2,1,0:T(8,128)(2,1)S(1)}, bf16[8,2,8,512]{3,2,1,0:T(8,128)(2,1)S(1)}, u32[]{:S(2)}, u32[]{:S(2)}) collective-permute-start(bf16[8,2,8,512]{3,2,1,0:T(8,128)(2,1)S(1)} %get-tuple-element.175), channel_id=1, source_target_pairs={{0,16},{8,24},{16,0},{24,8},{1,17},{9,25},{17,1},{25,9},{2,18},{10... | collective-permute-start | bytes 393224 | tf_op jit(solution)/shard_map/ppermute | solution.py:172
  165.7 1.8 collective-permute-start.59
  167.5 5.5 %collective-permute-done.78.refs_14_ = bf16[8,2,8,512]{3,2,1,0:T(8,128)(2,1)S(1)} collective-permute-done((bf16[8,2,8,512]{3,2,1,0:T(8,128)(2,1)S(1)}, bf16[8,2,8,512]{3,2,1,0:T(8,128)(2,1)S(1)}, u32[]{:S(2)}, u32[]{:S(2)}) %collective-permute-start.78) | collective-permute-done | bytes 131104 | tf_op jit(solution)/shard_map/ppermute | solution.py:172
  173.0 5.6 %collective-permute-done.58.refs_10_ = bf16[8,2,8,512]{3,2,1,0:T(8,128)(2,1)S(1)} collective-permute-done((bf16[8,2,8,512]{3,2,1,0:T(8,128)(2,1)S(1)}, bf16[8,2,8,512]{3,2,1,0:T(8,128)(2,1)S(1)}, u32[]{:S(2)}, u32[]{:S(2)}) %collective-permute-start.58) | collective-permute-done | bytes 131104 | tf_op jit(solution)/shard_map/ppermute | solution.py:172
  178.6 3.0 %unpack.1 = bf16[8,256,512]{2,1,0:T(8,128)(2,1)} custom-call(s32[2]{0:T(128)S(1)} %pad_add_fusion.place_ref, bf16[8,2,8,512]{3,2,1,0:T(8,128)(2,1)S(1)} %get-tuple-element.125.refs_0_, bf16[8,2,8,512]{3,2,1,0:T(8,128)(2,1)S(1)} %collective-permute-done.17.refs_1_, bf16[8,2,8,512]{3,2,1,0:T(8,128)(2,1)S(1)} %collective-permute-done.18.refs_2_, ...), custom_call_target="tpu_custom_call" | custom-call | bytes 4194304 | tf_op jit(solution)/shard_map/unpack/pallas_call | solution.py:243
  (157 shorter events, 58.9 us)
Async XLA Ops:
  3.0 12.9 %collective-permute-start.20 = (bf16[8,2,8,512]{3,2,1,0:T(8,128)(2,1)S(1)}, bf16[8,2,8,512]{3,2,1,0:T(8,128)(2,1)S(1)}, u32[]{:S(2)}, u32[]{:S(2)}) collective-permute-start(bf16[8,2,8,512]{3,2,1,0:T(8,128)(2,1)S(1)} %get-tuple-element.130), channel_id=1, source_target_pairs={{0,8},{8,0},{16,24},{24,16},{1,9},{9,1},{17,25},{25,17},{2,10},{10... | collective-permute-start | bytes 393224 | tf_op jit(solution)/shard_map/ppermute | solution.py:172
  6.1 12.9 %collective-permute-start.21 = (bf16[8,2,8,512]{3,2,1,0:T(8,128)(2,1)S(1)}, bf16[8,2,8,512]{3,2,1,0:T(8,128)(2,1)S(1)}, u32[]{:S(2)}, u32[]{:S(2)}) collective-permute-start(bf16[8,2,8,512]{3,2,1,0:T(8,128)(2,1)S(1)} %get-tuple-element.131), channel_id=1, source_target_pairs={{0,16},{8,24},{16,0},{24,8},{1,17},{9,25},{17,1},{25,9},{2,18},{10... | collective-permute-start | bytes 393224 | tf_op jit(solution)/shard_map/ppermute | solution.py:172
  8.7 11.8 %collective-permute-start.22 = (bf16[8,2,8,512]{3,2,1,0:T(8,128)(2,1)S(1)}, bf16[8,2,8,512]{3,2,1,0:T(8,128)(2,1)S(1)}, u32[]{:S(2)}, u32[]{:S(2)}) collective-permute-start(bf16[8,2,8,512]{3,2,1,0:T(8,128)(2,1)S(1)} %get-tuple-element.132), channel_id=1, source_target_pairs={{0,24},{8,16},{16,8},{24,0},{1,25},{9,17},{17,9},{25,1},{2,26},{10... | collective-permute-start | bytes 393224 | tf_op jit(solution)/shard_map/ppermute | solution.py:172
  10.1 19.5 %collective-permute-start = (bf16[8,2,8,512]{3,2,1,0:T(8,128)(2,1)S(1)}, bf16[8,2,8,512]{3,2,1,0:T(8,128)(2,1)S(1)}, u32[]{:S(2)}, u32[]{:S(2)}) collective-permute-start(bf16[8,2,8,512]{3,2,1,0:T(8,128)(2,1)S(1)} %get-tuple-element.106), channel_id=1, source_target_pairs={{0,8},{8,0},{16,24},{24,16},{1,9},{9,1},{17,25},{25,17},{2,10},{10... | collective-permute-start | bytes 393224 | tf_op jit(solution)/shard_map/ppermute | solution.py:172
  11.1 23.3 %collective-permute-start.1 = (bf16[8,2,8,512]{3,2,1,0:T(8,128)(2,1)S(1)}, bf16[8,2,8,512]{3,2,1,0:T(8,128)(2,1)S(1)}, u32[]{:S(2)}, u32[]{:S(2)}) collective-permute-start(bf16[8,2,8,512]{3,2,1,0:T(8,128)(2,1)S(1)} %get-tuple-element.107), channel_id=1, source_target_pairs={{0,16},{8,24},{16,0},{24,8},{1,17},{9,25},{17,1},{25,9},{2,18},{10... | collective-permute-start | bytes 393224 | tf_op jit(solution)/shard_map/ppermute | solution.py:172
  16.0 19.3 %collective-permute-start.2 = (bf16[8,2,8,512]{3,2,1,0:T(8,128)(2,1)S(1)}, bf16[8,2,8,512]{3,2,1,0:T(8,128)(2,1)S(1)}, u32[]{:S(2)}, u32[]{:S(2)}) collective-permute-start(bf16[8,2,8,512]{3,2,1,0:T(8,128)(2,1)S(1)} %get-tuple-element.108), channel_id=1, source_target_pairs={{0,24},{8,16},{16,8},{24,0},{1,25},{9,17},{17,9},{25,1},{2,26},{10... | collective-permute-start | bytes 393224 | tf_op jit(solution)/shard_map/ppermute | solution.py:172
  19.1 21.1 %collective-permute-start.60 = (bf16[8,2,8,512]{3,2,1,0:T(8,128)(2,1)S(1)}, bf16[8,2,8,512]{3,2,1,0:T(8,128)(2,1)S(1)}, u32[]{:S(2)}, u32[]{:S(2)}) collective-permute-start(bf16[8,2,8,512]{3,2,1,0:T(8,128)(2,1)S(1)} %get-tuple-element.178), channel_id=1, source_target_pairs={{0,8},{8,0},{16,24},{24,16},{1,9},{9,1},{17,25},{25,17},{2,10},{10... | collective-permute-start | bytes 393224 | tf_op jit(solution)/shard_map/ppermute | solution.py:172
  20.6 26.6 %collective-permute-start.61 = (bf16[8,2,8,512]{3,2,1,0:T(8,128)(2,1)S(1)}, bf16[8,2,8,512]{3,2,1,0:T(8,128)(2,1)S(1)}, u32[]{:S(2)}, u32[]{:S(2)}) collective-permute-start(bf16[8,2,8,512]{3,2,1,0:T(8,128)(2,1)S(1)} %get-tuple-element.179), channel_id=1, source_target_pairs={{0,16},{8,24},{16,0},{24,8},{1,17},{9,25},{17,1},{25,9},{2,18},{10... | collective-permute-start | bytes 393224 | tf_op jit(solution)/shard_map/ppermute | solution.py:172
  29.6 17.6 %collective-permute-start.62 = (bf16[8,2,8,512]{3,2,1,0:T(8,128)(2,1)S(1)}, bf16[8,2,8,512]{3,2,1,0:T(8,128)(2,1)S(1)}, u32[]{:S(2)}, u32[]{:S(2)}) collective-permute-start(bf16[8,2,8,512]{3,2,1,0:T(8,128)(2,1)S(1)} %get-tuple-element.180), channel_id=1, source_target_pairs={{0,24},{8,16},{16,8},{24,0},{1,25},{9,17},{17,9},{25,1},{2,26},{10... | collective-permute-start | bytes 393224 | tf_op jit(solution)/shard_map/ppermute | solution.py:172
  34.4 14.3 %collective-permute-start.40 = (bf16[8,2,8,512]{3,2,1,0:T(8,128)(2,1)S(1)}, bf16[8,2,8,512]{3,2,1,0:T(8,128)(2,1)S(1)}, u32[]{:S(2)}, u32[]{:S(2)}) collective-permute-start(bf16[8,2,8,512]{3,2,1,0:T(8,128)(2,1)S(1)} %get-tuple-element.154), channel_id=1, source_target_pairs={{0,8},{8,0},{16,24},{24,16},{1,9},{9,1},{17,25},{25,17},{2,10},{10... | collective-permute-start | bytes 393224 | tf_op jit(solution)/shard_map/ppermute | solution.py:172
  35.3 17.5 %collective-permute-start.41 = (bf16[8,2,8,512]{3,2,1,0:T(8,128)(2,1)S(1)}, bf16[8,2,8,512]{3,2,1,0:T(8,128)(2,1)S(1)}, u32[]{:S(2)}, u32[]{:S(2)}) collective-permute-start(bf16[8,2,8,512]{3,2,1,0:T(8,128)(2,1)S(1)} %get-tuple-element.155), channel_id=1, source_target_pairs={{0,16},{8,24},{16,0},{24,8},{1,17},{9,25},{17,1},{25,9},{2,18},{10... | collective-permute-start | bytes 393224 | tf_op jit(solution)/shard_map/ppermute | solution.py:172
  40.2 14.1 %collective-permute-start.42 = (bf16[8,2,8,512]{3,2,1,0:T(8,128)(2,1)S(1)}, bf16[8,2,8,512]{3,2,1,0:T(8,128)(2,1)S(1)}, u32[]{:S(2)}, u32[]{:S(2)}) collective-permute-start(bf16[8,2,8,512]{3,2,1,0:T(8,128)(2,1)S(1)} %get-tuple-element.156), channel_id=1, source_target_pairs={{0,24},{8,16},{16,8},{24,0},{1,25},{9,17},{17,9},{25,1},{2,26},{10... | collective-permute-start | bytes 393224 | tf_op jit(solution)/shard_map/ppermute | solution.py:172
  78.4 10.8 %collective-permute-start.46 = (bf16[2,32,512]{2,1,0:T(8,128)(2,1)S(1)}, bf16[2,32,512]{2,1,0:T(8,128)(2,1)S(1)}, u32[]{:S(2)}, u32[]{:S(2)}) collective-permute-start(bf16[2,32,512]{2,1,0:T(8,128)(2,1)S(1)} %get-tuple-element.161), channel_id=1, source_target_pairs={{0,4},{1,5},{2,6},{3,7},{4,0},{5,1},{6,2},{7,3},{8,12},{9,13},{10,... | collective-permute-start | bytes 196616 | tf_op jit(solution)/shard_map/ppermute | solution.py:172
  79.7 10.8 %collective-permute-start.47 = (bf16[2,32,512]{2,1,0:T(8,128)(2,1)S(1)}, bf16[2,32,512]{2,1,0:T(8,128)(2,1)S(1)}, u32[]{:S(2)}, u32[]{:S(2)}) collective-permute-start(bf16[2,32,512]{2,1,0:T(8,128)(2,1)S(1)} %get-tuple-element.162), channel_id=1, source_target_pairs={{0,5},{1,4},{2,7},{3,6},{4,1},{5,0},{6,3},{7,2},{8,13},{9,12},{10,... | collective-permute-start | bytes 196616 | tf_op jit(solution)/shard_map/ppermute | solution.py:172
  89.2 11.4 %collective-permute-start.31 = (bf16[2,32,512]{2,1,0:T(8,128)(2,1)S(1)}, bf16[2,32,512]{2,1,0:T(8,128)(2,1)S(1)}, u32[]{:S(2)}, u32[]{:S(2)}) collective-permute-start(bf16[2,32,512]{2,1,0:T(8,128)(2,1)S(1)} %get-tuple-element.143), channel_id=1, source_target_pairs={{0,2},{1,3},{2,0},{3,1},{4,6},{5,7},{6,4},{7,5},{8,10},{9,11},{10,... | collective-permute-start | bytes 196616 | tf_op jit(solution)/shard_map/ppermute | solution.py:172
  90.6 11.0 %collective-permute-start.33 = (bf16[2,32,512]{2,1,0:T(8,128)(2,1)S(1)}, bf16[2,32,512]{2,1,0:T(8,128)(2,1)S(1)}, u32[]{:S(2)}, u32[]{:S(2)}) collective-permute-start(bf16[2,32,512]{2,1,0:T(8,128)(2,1)S(1)} %get-tuple-element.145), channel_id=1, source_target_pairs={{0,4},{1,5},{2,6},{3,7},{4,0},{5,1},{6,2},{7,3},{8,12},{9,13},{10,... | collective-permute-start | bytes 196616 | tf_op jit(solution)/shard_map/ppermute | solution.py:172
  91.9 11.0 %collective-permute-start.34 = (bf16[2,32,512]{2,1,0:T(8,128)(2,1)S(1)}, bf16[2,32,512]{2,1,0:T(8,128)(2,1)S(1)}, u32[]{:S(2)}, u32[]{:S(2)}) collective-permute-start(bf16[2,32,512]{2,1,0:T(8,128)(2,1)S(1)} %get-tuple-element.146), channel_id=1, source_target_pairs={{0,5},{1,4},{2,7},{3,6},{4,1},{5,0},{6,3},{7,2},{8,13},{9,12},{10,... | collective-permute-start | bytes 196616 | tf_op jit(solution)/shard_map/ppermute | solution.py:172
  101.6 11.2 %collective-permute-start.11 = (bf16[2,32,512]{2,1,0:T(8,128)(2,1)S(1)}, bf16[2,32,512]{2,1,0:T(8,128)(2,1)S(1)}, u32[]{:S(2)}, u32[]{:S(2)}) collective-permute-start(bf16[2,32,512]{2,1,0:T(8,128)(2,1)S(1)} %get-tuple-element.119), channel_id=1, source_target_pairs={{0,2},{1,3},{2,0},{3,1},{4,6},{5,7},{6,4},{7,5},{8,10},{9,11},{10,... | collective-permute-start | bytes 196616 | tf_op jit(solution)/shard_map/ppermute | solution.py:172
  113.8 12.8 %collective-permute-start.71 = (bf16[2,32,512]{2,1,0:T(8,128)(2,1)S(1)}, bf16[2,32,512]{2,1,0:T(8,128)(2,1)S(1)}, u32[]{:S(2)}, u32[]{:S(2)}) collective-permute-start(bf16[2,32,512]{2,1,0:T(8,128)(2,1)S(1)} %get-tuple-element.191), channel_id=1, source_target_pairs={{0,2},{1,3},{2,0},{3,1},{4,6},{5,7},{6,4},{7,5},{8,10},{9,11},{10,... | collective-permute-start | bytes 196616 | tf_op jit(solution)/shard_map/ppermute | solution.py:172
  115.5 13.2 %collective-permute-start.72 = (bf16[2,32,512]{2,1,0:T(8,128)(2,1)S(1)}, bf16[2,32,512]{2,1,0:T(8,128)(2,1)S(1)}, u32[]{:S(2)}, u32[]{:S(2)}) collective-permute-start(bf16[2,32,512]{2,1,0:T(8,128)(2,1)S(1)} %get-tuple-element.192), channel_id=1, source_target_pairs={{0,3},{1,2},{2,1},{3,0},{4,7},{5,6},{6,5},{7,4},{8,11},{9,10},{10,... | collective-permute-start | bytes 196616 | tf_op jit(solution)/shard_map/ppermute | solution.py:172
  119.8 10.7 %collective-permute-start.75 = (bf16[2,32,512]{2,1,0:T(8,128)(2,1)S(1)}, bf16[2,32,512]{2,1,0:T(8,128)(2,1)S(1)}, u32[]{:S(2)}, u32[]{:S(2)}) collective-permute-start(bf16[2,32,512]{2,1,0:T(8,128)(2,1)S(1)} %get-tuple-element.195), channel_id=1, source_target_pairs={{0,6},{1,7},{2,4},{3,5},{4,2},{5,3},{6,0},{7,1},{8,14},{9,15},{10,... | collective-permute-start | bytes 196616 | tf_op jit(solution)/shard_map/ppermute | solution.py:172
  131.9 11.4 %collective-permute-start.37 = (bf16[8,2,8,512]{3,2,1,0:T(8,128)(2,1)S(1)}, bf16[8,2,8,512]{3,2,1,0:T(8,128)(2,1)S(1)}, u32[]{:S(2)}, u32[]{:S(2)}) collective-permute-start(bf16[8,2,8,512]{3,2,1,0:T(8,128)(2,1)S(1)} %get-tuple-element.150), channel_id=1, source_target_pairs={{0,8},{8,0},{16,24},{24,16},{1,9},{9,1},{17,25},{25,17},{2,10},{10... | collective-permute-start | bytes 393224 | tf_op jit(solution)/shard_map/ppermute | solution.py:172
  131.9 13.1 %collective-permute-start.38 = (bf16[8,2,8,512]{3,2,1,0:T(8,128)(2,1)S(1)}, bf16[8,2,8,512]{3,2,1,0:T(8,128)(2,1)S(1)}, u32[]{:S(2)}, u32[]{:S(2)}) collective-permute-start(bf16[8,2,8,512]{3,2,1,0:T(8,128)(2,1)S(1)} %get-tuple-element.151), channel_id=1, source_target_pairs={{0,16},{8,24},{16,0},{24,8},{1,17},{9,25},{17,1},{25,9},{2,18},{10... | collective-permute-start | bytes 393224 | tf_op jit(solution)/shard_map/ppermute | solution.py:172
  140.6 10.5 %collective-permute-start.17 = (bf16[8,2,8,512]{3,2,1,0:T(8,128)(2,1)S(1)}, bf16[8,2,8,512]{3,2,1,0:T(8,128)(2,1)S(1)}, u32[]{:S(2)}, u32[]{:S(2)}) collective-permute-start(bf16[8,2,8,512]{3,2,1,0:T(8,128)(2,1)S(1)} %get-tuple-element.126), channel_id=1, source_target_pairs={{0,8},{8,0},{16,24},{24,16},{1,9},{9,1},{17,25},{25,17},{2,10},{10... | collective-permute-start | bytes 393224 | tf_op jit(solution)/shard_map/ppermute | solution.py:172
  142.1 14.1 %collective-permute-start.18 = (bf16[8,2,8,512]{3,2,1,0:T(8,128)(2,1)S(1)}, bf16[8,2,8,512]{3,2,1,0:T(8,128)(2,1)S(1)}, u32[]{:S(2)}, u32[]{:S(2)}) collective-permute-start(bf16[8,2,8,512]{3,2,1,0:T(8,128)(2,1)S(1)} %get-tuple-element.127), channel_id=1, source_target_pairs={{0,16},{8,24},{16,0},{24,8},{1,17},{9,25},{17,1},{25,9},{2,18},{10... | collective-permute-start | bytes 393224 | tf_op jit(solution)/shard_map/ppermute | solution.py:172
  143.3 12.9 %collective-permute-start.19 = (bf16[8,2,8,512]{3,2,1,0:T(8,128)(2,1)S(1)}, bf16[8,2,8,512]{3,2,1,0:T(8,128)(2,1)S(1)}, u32[]{:S(2)}, u32[]{:S(2)}) collective-permute-start(bf16[8,2,8,512]{3,2,1,0:T(8,128)(2,1)S(1)} %get-tuple-element.128), channel_id=1, source_target_pairs={{0,24},{8,16},{16,8},{24,0},{1,25},{9,17},{17,9},{25,1},{2,26},{10... | collective-permute-start | bytes 393224 | tf_op jit(solution)/shard_map/ppermute | solution.py:172
  145.0 20.7 %collective-permute-start.77 = (bf16[8,2,8,512]{3,2,1,0:T(8,128)(2,1)S(1)}, bf16[8,2,8,512]{3,2,1,0:T(8,128)(2,1)S(1)}, u32[]{:S(2)}, u32[]{:S(2)}) collective-permute-start(bf16[8,2,8,512]{3,2,1,0:T(8,128)(2,1)S(1)} %get-tuple-element.198), channel_id=1, source_target_pairs={{0,8},{8,0},{16,24},{24,16},{1,9},{9,1},{17,25},{25,17},{2,10},{10... | collective-permute-start | bytes 393224 | tf_op jit(solution)/shard_map/ppermute | solution.py:172
  147.1 25.9 %collective-permute-start.78 = (bf16[8,2,8,512]{3,2,1,0:T(8,128)(2,1)S(1)}, bf16[8,2,8,512]{3,2,1,0:T(8,128)(2,1)S(1)}, u32[]{:S(2)}, u32[]{:S(2)}) collective-permute-start(bf16[8,2,8,512]{3,2,1,0:T(8,128)(2,1)S(1)} %get-tuple-element.199), channel_id=1, source_target_pairs={{0,16},{8,24},{16,0},{24,8},{1,17},{9,25},{17,1},{25,9},{2,18},{10... | collective-permute-start | bytes 393224 | tf_op jit(solution)/shard_map/ppermute | solution.py:172
  151.1 21.9 %collective-permute-start.79 = (bf16[8,2,8,512]{3,2,1,0:T(8,128)(2,1)S(1)}, bf16[8,2,8,512]{3,2,1,0:T(8,128)(2,1)S(1)}, u32[]{:S(2)}, u32[]{:S(2)}) collective-permute-start(bf16[8,2,8,512]{3,2,1,0:T(8,128)(2,1)S(1)} %get-tuple-element.200), channel_id=1, source_target_pairs={{0,24},{8,16},{16,8},{24,0},{1,25},{9,17},{17,9},{25,1},{2,26},{10... | collective-permute-start | bytes 393224 | tf_op jit(solution)/shard_map/ppermute | solution.py:172
  156.2 16.8 %collective-permute-start.57 = (bf16[8,2,8,512]{3,2,1,0:T(8,128)(2,1)S(1)}, bf16[8,2,8,512]{3,2,1,0:T(8,128)(2,1)S(1)}, u32[]{:S(2)}, u32[]{:S(2)}) collective-permute-start(bf16[8,2,8,512]{3,2,1,0:T(8,128)(2,1)S(1)} %get-tuple-element.174), channel_id=1, source_target_pairs={{0,8},{8,0},{16,24},{24,16},{1,9},{9,1},{17,25},{25,17},{2,10},{10... | collective-permute-start | bytes 393224 | tf_op jit(solution)/shard_map/ppermute | solution.py:172
  156.2 22.4 %collective-permute-start.58 = (bf16[8,2,8,512]{3,2,1,0:T(8,128)(2,1)S(1)}, bf16[8,2,8,512]{3,2,1,0:T(8,128)(2,1)S(1)}, u32[]{:S(2)}, u32[]{:S(2)}) collective-permute-start(bf16[8,2,8,512]{3,2,1,0:T(8,128)(2,1)S(1)} %get-tuple-element.175), channel_id=1, source_target_pairs={{0,16},{8,24},{16,0},{24,8},{1,17},{9,25},{17,1},{25,9},{2,18},{10... | collective-permute-start | bytes 393224 | tf_op jit(solution)/shard_map/ppermute | solution.py:172
  165.7 12.9 %collective-permute-start.59 = (bf16[8,2,8,512]{3,2,1,0:T(8,128)(2,1)S(1)}, bf16[8,2,8,512]{3,2,1,0:T(8,128)(2,1)S(1)}, u32[]{:S(2)}, u32[]{:S(2)}) collective-permute-start(bf16[8,2,8,512]{3,2,1,0:T(8,128)(2,1)S(1)} %get-tuple-element.176), channel_id=1, source_target_pairs={{0,24},{8,16},{16,8},{24,0},{1,25},{9,17},{17,9},{25,1},{2,26},{10... | collective-permute-start | bytes 393224 | tf_op jit(solution)/shard_map/ppermute | solution.py:172
  (53 other events, 571.5 us)

commit v2 on v1

v2 whole, which is shorter than its diff:
```python
import functools
import math

import jax
import jax.numpy as jnp
from jax import lax
from jax.experimental import pallas as pl
from jax.experimental.pallas import tpu as pltpu
from jax.sharding import PartitionSpec as P

OB = 128
ITERS = 6
LANES = 128
LONG = 10**11
VMEM = pl.BlockSpec(memory_space=pltpu.VMEM)
ANY = pl.BlockSpec(memory_space=pl.ANY)
SMEM = pl.BlockSpec(memory_space=pltpu.SMEM)
F32 = jnp.float32
BF16 = jnp.bfloat16
PARAMS = pltpu.CompilerParams(vmem_limit_bytes=40 * 2**20)


def cost(flops, touched):
    return pl.CostEstimate(flops=flops, bytes_accessed=touched, transcendentals=0)


def dot(left, right):
    return lax.dot_general(left, right, (((1,), (0,)), ((), ())), preferred_element_type=F32)


def dot_rows(left, right):
    return lax.dot_general(left, right, (((1,), (1,)), ((), ())), preferred_element_type=F32)


def split(value):
    high = value.astype(BF16)
    return high, (value - high.astype(F32)).astype(BF16)


def dot_split(left, right):
    return dot(
        jnp.concatenate([left[0], left[0], left[1]], axis=1),
        jnp.concatenate([right[0], right[1], right[0]], axis=0),
    )


def site_sums_kernel(states, blocks_ref, site_ref, precision_ref, innovation_ref, *refs):
    weight_ref, value_ref = refs[-2:]
    patches, slots = site_ref.shape
    groups = states // LANES
    rows = lax.broadcasted_iota(jnp.int32, (groups, slots), 0)
    lanes = lax.broadcasted_iota(jnp.int32, (LANES, slots), 0)
    slot = lax.broadcasted_iota(jnp.int32, (1, slots), 1)
    for patch in range(patches):
        sites = site_ref[patch : patch + 1, :]
        alive = slot < blocks_ref[patch] * OB
        live = jnp.where(alive, precision_ref[patch : patch + 1, :].astype(F32), 0.0)
        value = live * innovation_ref[patch : patch + 1, :].astype(F32)
        high = value.astype(BF16).astype(F32)
        picked = rows == sites // LANES
        left = jnp.concatenate(
            [jnp.where(picked, part, 0.0) for part in (live, high, value - high)], axis=0
        ).astype(BF16)
        right = jnp.where(lanes == sites % LANES, 1.0, 0.0).astype(BF16)
        sums = dot_rows(left, right)
        for group in range(groups):
            columns = slice(group * LANES, (group + 1) * LANES)
            weight_ref[patch : patch + 1, columns] = sums[group : group + 1]
            value_ref[patch : patch + 1, columns] = (
                sums[groups + group : groups + group + 1]
                + sums[2 * groups + group : 2 * groups + group + 1]
            )


def views(refs, size):
    return [refs[0].at[i] for i in range(size)] if len(refs) == 1 else list(refs)


def analyse_kernel(first, senders, receivers, taken, given, weight_ref, value_ref, *refs):
    ins, outs = views(refs[:taken], senders), views(refs[-given:], receivers)
    patches, part, states = ins[0].shape
    members = senders * part
    block = part // receivers
    grid_rows = lax.broadcasted_iota(jnp.int32, (members, members), 0)
    grid_columns = lax.broadcasted_iota(jnp.int32, (members, members), 1)
    eye = jnp.where(grid_rows == grid_columns, 1.0, 0.0)
    every = range(patches)

    means, perts, rests, scales, sides = [], [], [], [], []
    for patch in every:
        total = sum(jnp.sum(ref[patch].astype(F32), axis=0, keepdims=True) for ref in ins)
        mean = total / members
        pert = jnp.concatenate([(ref[patch].astype(F32) - mean).astype(BF16) for ref in ins], axis=0)
        weight = weight_ref[first + patch : first + patch + 1, :]
        value = value_ref[first + patch : first + patch + 1, :]
        scaled = split(pert.astype(F32) * weight)
        gram = dot_rows(jnp.concatenate(scaled, axis=1), jnp.concatenate([pert, pert], axis=1))
        sides.append(
            dot_rows(jnp.concatenate([jnp.broadcast_to(part_, (8, states)) for part_ in split(value)], axis=0), pert)
        )
        amat = (members - 1.0) * eye + gram
        square = jnp.sum(jnp.sum(amat * amat, axis=0, keepdims=True), axis=1, keepdims=True)
        scale = lax.rsqrt(square)
        means.append(mean)
        perts.append(pert)
        scales.append(scale)
        rests.append(eye - amat * scale)

    zs = [eye + 0.5 * rest for rest in rests]
    parts = [split(rest) for rest in rests]
    for step in range(1, ITERS):
        squares = [dot_split(part_, part_) for part_ in parts]
        halves = [split(0.25 * square) for square in squares]
        rests = [
            0.75 * square + dot_split(half, part_) for square, half, part_ in zip(squares, halves, parts)
        ]
        parts = [split(rest) for rest in rests]
        zs = [z + 0.5 * dot_split(part_, split(z)) for part_, z in zip(parts, zs)]

    for patch in every:
        z = split(zs[patch])
        row = sides[patch][0:1] + sides[patch][8:9]
        for _ in range(2):
            high, low = split(jnp.broadcast_to(row, (8, members)))
            row = (dot(high, z[0]) + (dot(high, z[1]) + dot(low, z[0])))[0:1]
        wmean = row * scales[patch]
        coef = wmean + (math.sqrt(members - 1.0) * lax.sqrt(scales[patch])) * zs[patch]
        update = dot(coef.astype(BF16), perts[patch])
        result = (means[patch] + update).astype(BF16)
        for sender in range(senders):
            for k, out in enumerate(outs):
                row_at = sender * part + k * block
                out[sender, patch] = result[row_at : row_at + block]


def pack_kernel(first, flip, seconds, firsts, given, place_ref, ensemble_ref, *refs):
    outs = views(refs[-given:], firsts)
    count = outs[0].shape[1]
    held = ensemble_ref.shape[1] // (firsts * seconds)
    regions = firsts if flip else seconds
    for f, out in enumerate(outs):
        def second(g, carry):
            k, j = (g, f) if flip else (f, g)
            owner = (place_ref[0] ^ k) * regions + j
            rows = pl.ds(pl.multiple_of(owner * held, held), held)
            block = ensemble_ref[:, rows, :].astype(F32)[:, first : first + count, :]
            out[g] = jnp.swapaxes(block, 0, 1).astype(BF16)
            return carry

        lax.fori_loop(0, seconds, second, 0)


def turn_kernel(firsts, seconds, taken, given, *refs):
    sources, outs = views(refs[:taken], firsts), views(refs[-given:], seconds)
    for g, out in enumerate(outs):
        for patch in range(out.shape[0]):
            out[patch] = jnp.concatenate([source[g, patch] for source in sources], axis=0)


def unpack_kernel(flips, regions, partners, place_ref, *refs):
    out = refs[-1]
    members = out.shape[0]
    held = out.shape[1] // (partners * regions)
    sources, at = [], 0
    for flip in flips:
        size = partners if flip else regions
        taken = partners if flip else 1
        sources.append(views(refs[at : at + taken], size))
        at += taken
    for k in range(partners):
        for j in range(regions):
            owner = (place_ref[0] ^ k) * regions + j
            rows = pl.ds(pl.multiple_of(owner * held, held), held)
            pieces = []
            for flip, arrays in zip(flips, sources):
                f, g = (j, k) if flip else (k, j)
                pieces.append(arrays[g][:, f * members : (f + 1) * members, :].astype(F32))
            out[:, rows, :] = jnp.swapaxes(jnp.concatenate(pieces, axis=0), 0, 1).astype(BF16)


def hold_kernel(*refs):
    refs[-1][...] = jnp.zeros_like(refs[-1])


def exchange(blocks, axis):
    if axis == "region":
        return [lax.all_to_all(blocks[0], axis, split_axis=0, concat_axis=0, tiled=True)]
    size = len(blocks)
    return [blocks[0]] + [
        lax.ppermute(blocks[k], axis, [(i, i ^ k) for i in range(size)]) for k in range(1, size)
    ]


def local(partners, regions, ensemble, obs_site, obs_blocks, obs_precision, obs_innovation):
    members, _, states = ensemble.shape
    held = obs_site.shape[0]
    place = lax.axis_index("member").astype(jnp.int32)[None]
    total = members * partners * regions
    flips = [False, True]
    counts = [held // 2, held - held // 2]
    starts = [0, held // 2]
    axes = [("member", "region"), ("region", "member")]
    sizes = [(partners, regions), (regions, partners)]
    last = [[]]
    state = {}

    def run(kernel, name, shapes, scalars, arrays, flops=0, touched=0):
        result = pl.pallas_call(
            kernel,
            out_shape=shapes,
            in_specs=[SMEM] * len(scalars) + [VMEM] * len(arrays) + [ANY] * len(last[0]),
            out_specs=[VMEM] * len(shapes),
            compiler_params=PARAMS,
            cost_estimate=cost(flops, touched),
            name=name,
        )(*scalars, *arrays, *last[0])
        last[0] = [result[0]]
        return result

    def blocks(axis, size, *shape):
        if axis == "region":
            return [jax.ShapeDtypeStruct((size,) + shape + (states,), BF16)]
        return [jax.ShapeDtypeStruct(shape + (states,), BF16)] * size

    def site_sums():
        sums = jax.ShapeDtypeStruct((held, states), F32)
        state["sums"] = run(
            functools.partial(site_sums_kernel, states), "site_sums", [sums, sums], [obs_blocks],
            [obs_site, obs_precision, obs_innovation],
        )

    def pack(c):
        first, second = sizes[c]
        shapes = blocks(axes[c][0], first, second, counts[c], members)
        packed = run(
            functools.partial(pack_kernel, starts[c], flips[c], second, first, len(shapes)), "pack",
            shapes, [place], [ensemble],
        )
        state[c] = exchange(packed, axes[c][0])

    def turn(c, flops=0):
        first, second = sizes[c]
        shapes = blocks(axes[c][1], second, counts[c], first * members)
        turned = run(
            functools.partial(turn_kernel, first, second, len(state[c]), len(shapes)), "turn",
            shapes, [], state[c], flops,
        )
        state[c] = exchange(turned, axes[c][1])

    def analyse(c):
        first, second = sizes[c]
        shapes = blocks(axes[c][0], first, second, counts[c], members)
        analysed = run(
            functools.partial(analyse_kernel, starts[c], second, first, len(state[c]), len(shapes)), "analyse",
            shapes, [], list(state["sums"]) + state[c],
            0,
        )
        state[c] = exchange(analysed, axes[c][0])

    def hold(c, flops):
        last[0] = last[0] + state[c]
        run(hold_kernel, "hold", [jax.ShapeDtypeStruct((8, LANES), F32)], [], [], flops)

    pack(0)
    pack(1)
    site_sums()
    turn(0, LONG)
    turn(1)
    analyse(0)
    analyse(1)
    turn(0, LONG)
    turn(1)
    hold(1, LONG)
    return run(
        functools.partial(unpack_kernel, flips, regions, partners), "unpack",
        [jax.ShapeDtypeStruct(ensemble.shape, BF16)], [place], state[0] + state[1],
    )[0]


def solution(mesh):
    placed = (
        P(("member", "region"), None, None),
        P(("member", "region"), None),
        P(("member", "region")),
        P(("member", "region"), None),
        P(("member", "region"), None),
    )
    return jax.shard_map(
        functools.partial(local, mesh.shape["member"], mesh.shape["region"]),
        mesh=mesh,
        in_specs=placed,
        out_specs=P(("member", "region"), None, None),
        check_vma=False,
    )
```

time: 182 us -> 119 us (0.65)
  starting transfers between devices: 108 us -> 36.2 us
  waiting for transfers between devices: 38.8 us -> 50.4 us
  Pallas kernels: 33.1 us -> 30.4 us
    ppermute x80 -> x12, starting transfers between devices: 108 us -> 21.6 us  [exchange(): lax.ppermute(blocks[k], axis, [(i, i ^ k) for i in range(size)])]
    all_to_all x0 -> x4, waiting for transfers between devices: none -> 23.8 us  [exchange(): lax.all_to_all(blocks[0], axis, split_axis=0, concat_axis=0, tiled=True)]
    all_to_all x0 -> x4, starting transfers between devices: none -> 14.6 us  [exchange(): lax.all_to_all(blocks[0], axis, split_axis=0, concat_axis=0, tiled=True)]
    ppermute x80 -> x12, waiting for transfers between devices: 38.8 us -> 26.6 us  [exchange(): lax.ppermute(blocks[k], axis, [(i, i ^ k) for i in range(size)])]
    pallas_call x18 -> x11, Pallas kernels: 33.1 us -> 30.4 us  [run(): pl.pallas_call(kernel, out_shape=shapes, in_specs=[SMEM] * len(scalars) +...]
  transfers between devices with their start and end apart: 80 -> 16, of which waited for: 16 -> 9; matrix products, arithmetic and copies ran while one was open for 0% -> 0% of each run, Pallas kernels for 16% -> 23%
where the time goes in v2:
time: 119 us
  waiting for transfers between devices  50.4 us (42%)
  starting transfers between devices  36.2 us (30%)
  Pallas kernels  30.4 us (26%)
  local copies, waits for them, and re-layouts  1.61 us (1%)
    pallas_call x11, Pallas kernels, run(): pl.pallas_call(kernel, out_shape=shapes, in_specs=[SMEM] * len(scalars) +...  30.4 us
    ppermute x12, waiting for transfers between devices, exchange(): lax.ppermute(blocks[k], axis, [(i, i ^ k) for i in range(size)])  26.6 us
    all_to_all x4, waiting for transfers between devices, exchange(): lax.all_to_all(blocks[0], axis, split_axis=0, concat_axis=0, tiled=True)  23.8 us
    ppermute x12, starting transfers between devices, exchange(): lax.ppermute(blocks[k], axis, [(i, i ^ k) for i in range(size)])  21.6 us
    all_to_all x4, starting transfers between devices, exchange(): lax.all_to_all(blocks[0], axis, split_axis=0, concat_axis=0, tiled=True)  14.6 us
  transfers between devices with their start and end apart: 16, of which 9 were waited for; matrix products, arithmetic and copies ran while one was open for 0% of the time, Pallas kernels for 23%

profile of v2, /device:TPU:0, one launch (start us, length us, event | category | flops | bytes accessed | tf_op | source)
XLA Modules:
  0.0 118.8 jit_solution(13428107718551763401)
XLA Ops:
  0.0 1.6 %copy-done = bf16[8,256,512]{2,1,0:T(8,128)(2,1)S(1)} copy-done((bf16[8,256,512]{2,1,0:T(8,128)(2,1)S(1)}, bf16[8,256,512]{2,1,0:T(8,128)(2,1)}, u32[]{:S(2)}) %copy-start) | copy-done | bytes 2097176
  1.6 0.8 pack.2
  2.4 3.1 %collective-permute-start = (bf16[8,4,8,512]{3,2,1,0:T(8,128)(2,1)S(1)}, bf16[8,4,8,512]{3,2,1,0:T(8,128)(2,1)S(1)}, u32[]{:S(2)}, u32[]{:S(2)}) collective-permute-start(bf16[8,4,8,512]{3,2,1,0:T(8,128)(2,1)S(1)} %get-tuple-element.26), channel_id=1, source_target_pairs={{0,8},{8,0},{16,24},{24,16},{1,9},{9,1},{17,25},{25,17},{2,10},{10... | collective-permute-start | bytes 786440 | tf_op jit(solution)/shard_map/ppermute | solution.py:190
  5.5 2.6 %collective-permute-start.1 = (bf16[8,4,8,512]{3,2,1,0:T(8,128)(2,1)S(1)}, bf16[8,4,8,512]{3,2,1,0:T(8,128)(2,1)S(1)}, u32[]{:S(2)}, u32[]{:S(2)}) collective-permute-start(bf16[8,4,8,512]{3,2,1,0:T(8,128)(2,1)S(1)} %get-tuple-element.27), channel_id=1, source_target_pairs={{0,16},{8,24},{16,0},{24,8},{1,17},{9,25},{17,1},{25,9},{2,18},{10... | collective-permute-start | bytes 786440 | tf_op jit(solution)/shard_map/ppermute | solution.py:190
  8.1 1.8 %pack.3.refs_0_ = bf16[8,4,4,8,512]{4,3,2,1,0:T(8,128)(2,1)} custom-call(s32[1]{0:T(128)} %bitcast.place_ref, bf16[8,256,512]{2,1,0:T(8,128)(2,1)S(1)} %copy-done, bf16[8,4,8,512]{3,2,1,0:T(8,128)(2,1)S(1)} %get-tuple-element.23.refs_0_), custom_call_target="tpu_custom_call" | custom-call | tf_op jit(solution)/shard_map/pack/pallas_call | solution.py:208
  9.9 3.9 %all-to-all-start.1 = ((bf16[8,4,4,8,512]{4,3,2,1,0:T(8,128)(2,1)}), bf16[8,4,4,8,512]{4,3,2,1,0:T(8,128)(2,1)S(1)}, u32[]{:S(2)}, u32[]{:S(2)}) async-start(bf16[8,4,4,8,512]{4,3,2,1,0:T(8,128)(2,1)} %pack.3.refs_0_), calls=%async_computation.1 | async-start | bytes 2097152 | tf_op jit(solution)/shard_map/all_to_all | solution.py:187
  13.9 1.7 %site_sums.1 = (f32[8,512]{1,0:T(8,128)S(1)}, f32[8,512]{1,0:T(8,128)S(1)}) custom-call(s32[8]{0:T(128)S(1)} %copy-done.4, s32[8,2048]{1,0:T(8,128)S(1)} %copy-done.1, bf16[8,2048]{1,0:T(8,128)(2,1)S(1)} %copy-done.2, bf16[8,2048]{1,0:T(8,128)(2,1)S(1)} %copy-done.3, bf16[8,4,4,8,512]{4,3,2,1,0:T(8,128)(2,1)} %pack.3.refs_0_), custom_call_target="tpu_custom_call" | custom-call | tf_op jit(solution)/shard_map/site_sums/pallas_call | solution.py:208
  15.6 1.0 collective-permute-done.refs_1_
  16.7 10.2 %collective-permute-done.1.refs_2_ = bf16[8,4,8,512]{3,2,1,0:T(8,128)(2,1)S(1)} collective-permute-done((bf16[8,4,8,512]{3,2,1,0:T(8,128)(2,1)S(1)}, bf16[8,4,8,512]{3,2,1,0:T(8,128)(2,1)S(1)}, u32[]{:S(2)}, u32[]{:S(2)}) %collective-permute-start.1) | collective-permute-done | bytes 262176 | tf_op jit(solution)/shard_map/ppermute | solution.py:190
  26.9 1.2 turn.4.refs_1_
  28.0 1.2 %all-to-all-done.1.refs_0_ = bf16[8,4,4,8,512]{4,3,2,1,0:T(8,128)(2,1)S(1)} async-done(((bf16[8,4,4,8,512]{4,3,2,1,0:T(8,128)(2,1)}), bf16[8,4,4,8,512]{4,3,2,1,0:T(8,128)(2,1)S(1)}, u32[]{:S(2)}, u32[]{:S(2)}) %all-to-all-start.1) | async-done | bytes 1048608 | tf_op jit(solution)/shard_map/all_to_all | solution.py:187
  29.3 3.6 %all-to-all-start = ((bf16[8,4,32,512]{3,2,1,0:T(8,128)(2,1)}), bf16[8,4,32,512]{3,2,1,0:T(8,128)(2,1)S(1)}, u32[]{:S(2)}, u32[]{:S(2)}) async-start(bf16[8,4,32,512]{3,2,1,0:T(8,128)(2,1)} %turn.4.refs_1_), calls=%async_computation | async-start | bytes 2097152 | tf_op jit(solution)/shard_map/all_to_all | solution.py:187
  32.8 0.8 turn.5
  33.6 3.7 %collective-permute-start.6 = (bf16[4,64,512]{2,1,0:T(8,128)(2,1)}, bf16[4,64,512]{2,1,0:T(8,128)(2,1)S(1)}, u32[]{:S(2)}, u32[]{:S(2)}) collective-permute-start(bf16[4,64,512]{2,1,0:T(8,128)(2,1)} %get-tuple-element.34), channel_id=1, source_target_pairs={{0,8},{8,0},{16,24},{24,16},{1,9},{9,1},{17,25},{25,17},{2,10},{10... | collective-permute-start | bytes 786440 | tf_op jit(solution)/shard_map/ppermute | solution.py:190
  37.3 1.0 collective-permute-start.7
  38.3 1.5 %collective-permute-start.8 = (bf16[4,64,512]{2,1,0:T(8,128)(2,1)S(1)}, bf16[4,64,512]{2,1,0:T(8,128)(2,1)S(1)}, u32[]{:S(2)}, u32[]{:S(2)}) collective-permute-start(bf16[4,64,512]{2,1,0:T(8,128)(2,1)S(1)} %get-tuple-element.36), channel_id=1, source_target_pairs={{0,24},{8,16},{16,8},{24,0},{1,25},{9,17},{17,9},{25,1},{2,26},{10... | collective-permute-start | bytes 786440 | tf_op jit(solution)/shard_map/ppermute | solution.py:190
  39.8 8.4 %all-to-all-done.refs_0_ = bf16[8,4,32,512]{3,2,1,0:T(8,128)(2,1)S(1)} async-done(((bf16[8,4,32,512]{3,2,1,0:T(8,128)(2,1)}), bf16[8,4,32,512]{3,2,1,0:T(8,128)(2,1)S(1)}, u32[]{:S(2)}, u32[]{:S(2)}) %all-to-all-start) | async-done | bytes 1048608 | tf_op jit(solution)/shard_map/all_to_all | solution.py:187
  48.2 10.1 %analyse.2 = (bf16[8,4,8,512]{3,2,1,0:T(8,128)(2,1)S(1)}, bf16[8,4,8,512]{3,2,1,0:T(8,128)(2,1)}, bf16[8,4,8,512]{3,2,1,0:T(8,128)(2,1)}, bf16[8,4,8,512]{3,2,1,0:T(8,128)(2,1)S(1)}) custom-call(f32[8,512]{1,0:T(8,128)S(1)} %get-tuple-element.24.refs_4_.weight_ref, f32[8,512]{1,0:T(8,128)S(1)} %get-tuple-element.25.value_ref, ...), custom_call_target="tpu_custom_call" | custom-call | tf_op jit(solution)/shard_map/analyse/pallas_call | solution.py:208
  58.3 3.8 %collective-permute-start.3 = (bf16[8,4,8,512]{3,2,1,0:T(8,128)(2,1)}, bf16[8,4,8,512]{3,2,1,0:T(8,128)(2,1)S(1)}, u32[]{:S(2)}, u32[]{:S(2)}) collective-permute-start(bf16[8,4,8,512]{3,2,1,0:T(8,128)(2,1)} %get-tuple-element.31), channel_id=1, source_target_pairs={{0,8},{8,0},{16,24},{24,16},{1,9},{9,1},{17,25},{25,17},{2,10},{10... | collective-permute-start | bytes 786440 | tf_op jit(solution)/shard_map/ppermute | solution.py:190
  62.0 1.0 collective-permute-start.4
  63.1 1.5 %collective-permute-start.5 = (bf16[8,4,8,512]{3,2,1,0:T(8,128)(2,1)S(1)}, bf16[8,4,8,512]{3,2,1,0:T(8,128)(2,1)S(1)}, u32[]{:S(2)}, u32[]{:S(2)}) collective-permute-start(bf16[8,4,8,512]{3,2,1,0:T(8,128)(2,1)S(1)} %get-tuple-element.33), channel_id=1, source_target_pairs={{0,24},{8,16},{16,8},{24,0},{1,25},{9,17},{17,9},{25,1},{2,26},{10... | collective-permute-start | bytes 786440 | tf_op jit(solution)/shard_map/ppermute | solution.py:190
  64.5 10.5 %analyse.3.refs_4_ = bf16[8,4,4,8,512]{4,3,2,1,0:T(8,128)(2,1)} custom-call(f32[8,512]{1,0:T(8,128)S(1)} %get-tuple-element.24.refs_4_.weight_ref, f32[8,512]{1,0:T(8,128)S(1)} %get-tuple-element.25.value_ref, bf16[4,64,512]{2,1,0:T(8,128)(2,1)S(1)} %get-tuple-element.29.refs_1_.refs_0_, bf16[4,64,512]{2,1,0:T(8,128)(2,1)S(1)} %collective-permute-done.6.refs_1_, ...), custom_call_target="tpu_custom_call" | custom-call | tf_op jit(solution)/shard_map/analyse/pallas_call | solution.py:208
  75.0 3.6 %all-to-all-start.3 = ((bf16[8,4,4,8,512]{4,3,2,1,0:T(8,128)(2,1)}), bf16[8,4,4,8,512]{4,3,2,1,0:T(8,128)(2,1)S(1)}, u32[]{:S(2)}, u32[]{:S(2)}) async-start(bf16[8,4,4,8,512]{4,3,2,1,0:T(8,128)(2,1)} %analyse.3.refs_4_), calls=%async_computation.3 | async-start | bytes 2097152 | tf_op jit(solution)/shard_map/all_to_all | solution.py:187
  78.6 3.7 %collective-permute-done.4.refs_2_ = bf16[8,4,8,512]{3,2,1,0:T(8,128)(2,1)S(1)} collective-permute-done((bf16[8,4,8,512]{3,2,1,0:T(8,128)(2,1)}, bf16[8,4,8,512]{3,2,1,0:T(8,128)(2,1)S(1)}, u32[]{:S(2)}, u32[]{:S(2)}) %collective-permute-start.4) | collective-permute-done | bytes 262176 | tf_op jit(solution)/shard_map/ppermute | solution.py:190
  82.3 1.1 turn.6.refs_1_
  83.4 10.4 %all-to-all-done.3.refs_0_ = bf16[8,4,4,8,512]{4,3,2,1,0:T(8,128)(2,1)S(1)} async-done(((bf16[8,4,4,8,512]{4,3,2,1,0:T(8,128)(2,1)}), bf16[8,4,4,8,512]{4,3,2,1,0:T(8,128)(2,1)S(1)}, u32[]{:S(2)}, u32[]{:S(2)}) %all-to-all-start.3) | async-done | bytes 1048608 | tf_op jit(solution)/shard_map/all_to_all | solution.py:187
  94.0 2.6 %collective-permute-start.10 = (bf16[4,64,512]{2,1,0:T(8,128)(2,1)S(1)}, bf16[4,64,512]{2,1,0:T(8,128)(2,1)S(1)}, u32[]{:S(2)}, u32[]{:S(2)}) collective-permute-start(bf16[4,64,512]{2,1,0:T(8,128)(2,1)S(1)} %get-tuple-element.39), channel_id=1, source_target_pairs={{0,16},{8,24},{16,0},{24,8},{1,17},{9,25},{17,1},{25,9},{2,18},{10... | collective-permute-start | bytes 786440 | tf_op jit(solution)/shard_map/ppermute | solution.py:190
  96.7 0.8 collective-permute-start.11
  97.6 3.6 %all-to-all-start.2 = ((bf16[8,4,32,512]{3,2,1,0:T(8,128)(2,1)}), bf16[8,4,32,512]{3,2,1,0:T(8,128)(2,1)S(1)}, u32[]{:S(2)}, u32[]{:S(2)}) async-start(bf16[8,4,32,512]{3,2,1,0:T(8,128)(2,1)} %turn.6.refs_1_), calls=%async_computation.2 | async-start | bytes 2097152 | tf_op jit(solution)/shard_map/all_to_all | solution.py:187
  101.2 10.9 %collective-permute-done.10.refs_3_ = bf16[4,64,512]{2,1,0:T(8,128)(2,1)S(1)} collective-permute-done((bf16[4,64,512]{2,1,0:T(8,128)(2,1)S(1)}, bf16[4,64,512]{2,1,0:T(8,128)(2,1)S(1)}, u32[]{:S(2)}, u32[]{:S(2)}) %collective-permute-start.10) | collective-permute-done | bytes 262176 | tf_op jit(solution)/shard_map/ppermute | solution.py:190
  112.8 3.7 %all-to-all-done.2.refs_0_ = bf16[8,4,32,512]{3,2,1,0:T(8,128)(2,1)S(1)} async-done(((bf16[8,4,32,512]{3,2,1,0:T(8,128)(2,1)}), bf16[8,4,32,512]{3,2,1,0:T(8,128)(2,1)S(1)}, u32[]{:S(2)}, u32[]{:S(2)}) %all-to-all-start.2) | async-done | bytes 1048608 | tf_op jit(solution)/shard_map/all_to_all | solution.py:187
  116.5 2.3 %unpack.1 = bf16[8,256,512]{2,1,0:T(8,128)(2,1)} custom-call(s32[1]{0:T(128)} %bitcast.place_ref, bf16[8,4,32,512]{3,2,1,0:T(8,128)(2,1)S(1)} %all-to-all-done.2.refs_0_, bf16[4,64,512]{2,1,0:T(8,128)(2,1)S(1)} %get-tuple-element.37.refs_0_.refs_1_, bf16[4,64,512]{2,1,0:T(8,128)(2,1)S(1)} %collective-permute-done.9.refs_2_, ...), custom_call_target="tpu_custom_call" | custom-call | tf_op jit(solution)/shard_map/unpack/pallas_call | solution.py:208
  (21 shorter events, 1.0 us)
Async XLA Ops:
  0.0 1.6 %copy-start = (bf16[8,256,512]{2,1,0:T(8,128)(2,1)S(1)}, bf16[8,256,512]{2,1,0:T(8,128)(2,1)}, u32[]{:S(2)}) copy-start(bf16[8,256,512]{2,1,0:T(8,128)(2,1)} %ensemble_ref.3) | copy-start | bytes 6291460
  2.4 14.2 %collective-permute-start = (bf16[8,4,8,512]{3,2,1,0:T(8,128)(2,1)S(1)}, bf16[8,4,8,512]{3,2,1,0:T(8,128)(2,1)S(1)}, u32[]{:S(2)}, u32[]{:S(2)}) collective-permute-start(bf16[8,4,8,512]{3,2,1,0:T(8,128)(2,1)S(1)} %get-tuple-element.26), channel_id=1, source_target_pairs={{0,8},{8,0},{16,24},{24,16},{1,9},{9,1},{17,25},{25,17},{2,10},{10... | collective-permute-start | bytes 786440 | tf_op jit(solution)/shard_map/ppermute | solution.py:190
  5.5 21.4 %collective-permute-start.1 = (bf16[8,4,8,512]{3,2,1,0:T(8,128)(2,1)S(1)}, bf16[8,4,8,512]{3,2,1,0:T(8,128)(2,1)S(1)}, u32[]{:S(2)}, u32[]{:S(2)}) collective-permute-start(bf16[8,4,8,512]{3,2,1,0:T(8,128)(2,1)S(1)} %get-tuple-element.27), channel_id=1, source_target_pairs={{0,16},{8,24},{16,0},{24,8},{1,17},{9,25},{17,1},{25,9},{2,18},{10... | collective-permute-start | bytes 786440 | tf_op jit(solution)/shard_map/ppermute | solution.py:190
  8.1 18.8 %collective-permute-start.2 = (bf16[8,4,8,512]{3,2,1,0:T(8,128)(2,1)S(1)}, bf16[8,4,8,512]{3,2,1,0:T(8,128)(2,1)S(1)}, u32[]{:S(2)}, u32[]{:S(2)}) collective-permute-start(bf16[8,4,8,512]{3,2,1,0:T(8,128)(2,1)S(1)} %get-tuple-element.28), channel_id=1, source_target_pairs={{0,24},{8,16},{16,8},{24,0},{1,25},{9,17},{17,9},{25,1},{2,26},{10... | collective-permute-start | bytes 786440 | tf_op jit(solution)/shard_map/ppermute | solution.py:190
  8.1 5.8 %copy-start.1 = (s32[8,2048]{1,0:T(8,128)S(1)}, s32[8,2048]{1,0:T(8,128)}, u32[]{:S(2)}) copy-start(s32[8,2048]{1,0:T(8,128)} %site_ref.1) | copy-start | bytes 196612
  8.1 5.8 %copy-start.2 = (bf16[8,2048]{1,0:T(8,128)(2,1)S(1)}, bf16[8,2048]{1,0:T(8,128)(2,1)}, u32[]{:S(2)}) copy-start(bf16[8,2048]{1,0:T(8,128)(2,1)} %precision_ref.1) | copy-start | bytes 98308
  8.1 5.8 %copy-start.3 = (bf16[8,2048]{1,0:T(8,128)(2,1)S(1)}, bf16[8,2048]{1,0:T(8,128)(2,1)}, u32[]{:S(2)}) copy-start(bf16[8,2048]{1,0:T(8,128)(2,1)} %innovation_ref.1) | copy-start | bytes 98308
  8.1 5.8 %copy-start.4 = (s32[8]{0:T(128)S(1)}, s32[8]{0:T(128)}, u32[]{:S(2)}) copy-start(s32[8]{0:T(128)} %blocks_ref.1) | copy-start | bytes 100
  9.9 19.3 %all-to-all-start.1 = ((bf16[8,4,4,8,512]{4,3,2,1,0:T(8,128)(2,1)}), bf16[8,4,4,8,512]{4,3,2,1,0:T(8,128)(2,1)S(1)}, u32[]{:S(2)}, u32[]{:S(2)}) async-start(bf16[8,4,4,8,512]{4,3,2,1,0:T(8,128)(2,1)} %pack.3.refs_0_), calls=%async_computation.1 | async-start | bytes 2097152 | tf_op jit(solution)/shard_map/all_to_all | solution.py:187
  29.3 18.9 %all-to-all-start = ((bf16[8,4,32,512]{3,2,1,0:T(8,128)(2,1)}), bf16[8,4,32,512]{3,2,1,0:T(8,128)(2,1)S(1)}, u32[]{:S(2)}, u32[]{:S(2)}) async-start(bf16[8,4,32,512]{3,2,1,0:T(8,128)(2,1)} %turn.4.refs_1_), calls=%async_computation | async-start | bytes 2097152 | tf_op jit(solution)/shard_map/all_to_all | solution.py:187
  33.6 29.4 %collective-permute-start.6 = (bf16[4,64,512]{2,1,0:T(8,128)(2,1)}, bf16[4,64,512]{2,1,0:T(8,128)(2,1)S(1)}, u32[]{:S(2)}, u32[]{:S(2)}) collective-permute-start(bf16[4,64,512]{2,1,0:T(8,128)(2,1)} %get-tuple-element.34), channel_id=1, source_target_pairs={{0,8},{8,0},{16,24},{24,16},{1,9},{9,1},{17,25},{25,17},{2,10},{10... | collective-permute-start | bytes 786440 | tf_op jit(solution)/shard_map/ppermute | solution.py:190
  37.3 27.2 %collective-permute-start.7 = (bf16[4,64,512]{2,1,0:T(8,128)(2,1)S(1)}, bf16[4,64,512]{2,1,0:T(8,128)(2,1)S(1)}, u32[]{:S(2)}, u32[]{:S(2)}) collective-permute-start(bf16[4,64,512]{2,1,0:T(8,128)(2,1)S(1)} %get-tuple-element.35), channel_id=1, source_target_pairs={{0,16},{8,24},{16,0},{24,8},{1,17},{9,25},{17,1},{25,9},{2,18},{10... | collective-permute-start | bytes 786440 | tf_op jit(solution)/shard_map/ppermute | solution.py:190
  38.3 26.2 %collective-permute-start.8 = (bf16[4,64,512]{2,1,0:T(8,128)(2,1)S(1)}, bf16[4,64,512]{2,1,0:T(8,128)(2,1)S(1)}, u32[]{:S(2)}, u32[]{:S(2)}) collective-permute-start(bf16[4,64,512]{2,1,0:T(8,128)(2,1)S(1)} %get-tuple-element.36), channel_id=1, source_target_pairs={{0,24},{8,16},{16,8},{24,0},{1,25},{9,17},{17,9},{25,1},{2,26},{10... | collective-permute-start | bytes 786440 | tf_op jit(solution)/shard_map/ppermute | solution.py:190
  58.3 20.3 %collective-permute-start.3 = (bf16[8,4,8,512]{3,2,1,0:T(8,128)(2,1)}, bf16[8,4,8,512]{3,2,1,0:T(8,128)(2,1)S(1)}, u32[]{:S(2)}, u32[]{:S(2)}) collective-permute-start(bf16[8,4,8,512]{3,2,1,0:T(8,128)(2,1)} %get-tuple-element.31), channel_id=1, source_target_pairs={{0,8},{8,0},{16,24},{24,16},{1,9},{9,1},{17,25},{25,17},{2,10},{10... | collective-permute-start | bytes 786440 | tf_op jit(solution)/shard_map/ppermute | solution.py:190
  62.0 20.3 %collective-permute-start.4 = (bf16[8,4,8,512]{3,2,1,0:T(8,128)(2,1)}, bf16[8,4,8,512]{3,2,1,0:T(8,128)(2,1)S(1)}, u32[]{:S(2)}, u32[]{:S(2)}) collective-permute-start(bf16[8,4,8,512]{3,2,1,0:T(8,128)(2,1)} %get-tuple-element.32), channel_id=1, source_target_pairs={{0,16},{8,24},{16,0},{24,8},{1,17},{9,25},{17,1},{25,9},{2,18},{10... | collective-permute-start | bytes 786440 | tf_op jit(solution)/shard_map/ppermute | solution.py:190
  63.1 19.3 %collective-permute-start.5 = (bf16[8,4,8,512]{3,2,1,0:T(8,128)(2,1)S(1)}, bf16[8,4,8,512]{3,2,1,0:T(8,128)(2,1)S(1)}, u32[]{:S(2)}, u32[]{:S(2)}) collective-permute-start(bf16[8,4,8,512]{3,2,1,0:T(8,128)(2,1)S(1)} %get-tuple-element.33), channel_id=1, source_target_pairs={{0,24},{8,16},{16,8},{24,0},{1,25},{9,17},{17,9},{25,1},{2,26},{10... | collective-permute-start | bytes 786440 | tf_op jit(solution)/shard_map/ppermute | solution.py:190
  75.0 18.9 %all-to-all-start.3 = ((bf16[8,4,4,8,512]{4,3,2,1,0:T(8,128)(2,1)}), bf16[8,4,4,8,512]{4,3,2,1,0:T(8,128)(2,1)S(1)}, u32[]{:S(2)}, u32[]{:S(2)}) async-start(bf16[8,4,4,8,512]{4,3,2,1,0:T(8,128)(2,1)} %analyse.3.refs_4_), calls=%async_computation.3 | async-start | bytes 2097152 | tf_op jit(solution)/shard_map/all_to_all | solution.py:187
  94.0 18.0 %collective-permute-start.10 = (bf16[4,64,512]{2,1,0:T(8,128)(2,1)S(1)}, bf16[4,64,512]{2,1,0:T(8,128)(2,1)S(1)}, u32[]{:S(2)}, u32[]{:S(2)}) collective-permute-start(bf16[4,64,512]{2,1,0:T(8,128)(2,1)S(1)} %get-tuple-element.39), channel_id=1, source_target_pairs={{0,16},{8,24},{16,0},{24,8},{1,17},{9,25},{17,1},{25,9},{2,18},{10... | collective-permute-start | bytes 786440 | tf_op jit(solution)/shard_map/ppermute | solution.py:190
  96.7 15.4 %collective-permute-start.11 = (bf16[4,64,512]{2,1,0:T(8,128)(2,1)S(1)}, bf16[4,64,512]{2,1,0:T(8,128)(2,1)S(1)}, u32[]{:S(2)}, u32[]{:S(2)}) collective-permute-start(bf16[4,64,512]{2,1,0:T(8,128)(2,1)S(1)} %get-tuple-element.40), channel_id=1, source_target_pairs={{0,24},{8,16},{16,8},{24,0},{1,25},{9,17},{17,9},{25,1},{2,26},{10... | collective-permute-start | bytes 786440 | tf_op jit(solution)/shard_map/ppermute | solution.py:190
  97.5 15.3 %collective-permute-start.9 = (bf16[4,64,512]{2,1,0:T(8,128)(2,1)S(1)}, bf16[4,64,512]{2,1,0:T(8,128)(2,1)S(1)}, u32[]{:S(2)}, u32[]{:S(2)}) collective-permute-start(bf16[4,64,512]{2,1,0:T(8,128)(2,1)S(1)} %get-tuple-element.38), channel_id=1, source_target_pairs={{0,8},{8,0},{16,24},{24,16},{1,9},{9,1},{17,25},{25,17},{2,10},{10... | collective-permute-start | bytes 786440 | tf_op jit(solution)/shard_map/ppermute | solution.py:190
  97.6 18.9 %all-to-all-start.2 = ((bf16[8,4,32,512]{3,2,1,0:T(8,128)(2,1)}), bf16[8,4,32,512]{3,2,1,0:T(8,128)(2,1)S(1)}, u32[]{:S(2)}, u32[]{:S(2)}) async-start(bf16[8,4,32,512]{3,2,1,0:T(8,128)(2,1)} %turn.6.refs_1_), calls=%async_computation.2 | async-start | bytes 2097152 | tf_op jit(solution)/shard_map/all_to_all | solution.py:187

commit v3 on v2

--- a/solution.py
+++ b/solution.py
@@ -12,6 +12,7 @@
 ITERS = 6
 LANES = 128
 LONG = 10**11
+SHORT = 10**10
 VMEM = pl.BlockSpec(memory_space=pltpu.VMEM)
 ANY = pl.BlockSpec(memory_space=pl.ANY)
 SMEM = pl.BlockSpec(memory_space=pltpu.SMEM)
@@ -76,11 +77,12 @@
     return [refs[0].at[i] for i in range(size)] if len(refs) == 1 else list(refs)
 
 
-def analyse_kernel(first, senders, receivers, taken, given, weight_ref, value_ref, *refs):
-    ins, outs = views(refs[:taken], senders), views(refs[-given:], receivers)
+def analyse_kernel(first, senders, taken, weight_ref, value_ref, *refs):
+    ins, outs = views(refs[:taken], senders), views(refs[-taken:], senders)
     patches, part, states = ins[0].shape
     members = senders * part
-    block = part // receivers
+    blocks = outs[0].shape[0]
+    block = part // blocks
     grid_rows = lax.broadcasted_iota(jnp.int32, (members, members), 0)
     grid_columns = lax.broadcasted_iota(jnp.int32, (members, members), 1)
     eye = jnp.where(grid_rows == grid_columns, 1.0, 0.0)
@@ -93,11 +95,10 @@
         pert = jnp.concatenate([(ref[patch].astype(F32) - mean).astype(BF16) for ref in ins], axis=0)
         weight = weight_ref[first + patch : first + patch + 1, :]
         value = value_ref[first + patch : first + patch + 1, :]
-        scaled = split(pert.astype(F32) * weight)
+        wide = pert.astype(F32)
+        scaled = split(wide * weight)
         gram = dot_rows(jnp.concatenate(scaled, axis=1), jnp.concatenate([pert, pert], axis=1))
-        sides.append(
-            dot_rows(jnp.concatenate([jnp.broadcast_to(part_, (8, states)) for part_ in split(value)], axis=0), pert)
-        )
+        sides.append(jnp.sum(wide * value, axis=1, keepdims=True))
         amat = (members - 1.0) * eye + gram
         square = jnp.sum(jnp.sum(amat * amat, axis=0, keepdims=True), axis=1, keepdims=True)
         scale = lax.rsqrt(square)
@@ -119,18 +120,16 @@
 
     for patch in every:
         z = split(zs[patch])
-        row = sides[patch][0:1] + sides[patch][8:9]
-        for _ in range(2):
-            high, low = split(jnp.broadcast_to(row, (8, members)))
-            row = (dot(high, z[0]) + (dot(high, z[1]) + dot(low, z[0])))[0:1]
-        wmean = row * scales[patch]
+        row = split(jnp.broadcast_to(jnp.sum(sides[patch] * zs[patch], axis=0, keepdims=True), (8, members)))
+        both = dot(jnp.concatenate(row, axis=0), z[0])
+        wmean = (both[0:1] + (both[8:9] + dot(row[0], z[1])[0:1])) * scales[patch]
         coef = wmean + (math.sqrt(members - 1.0) * lax.sqrt(scales[patch])) * zs[patch]
         update = dot(coef.astype(BF16), perts[patch])
         result = (means[patch] + update).astype(BF16)
-        for sender in range(senders):
-            for k, out in enumerate(outs):
+        for sender, out in enumerate(outs):
+            for k in range(blocks):
                 row_at = sender * part + k * block
-                out[sender, patch] = result[row_at : row_at + block]
+                out[k, patch] = result[row_at : row_at + block]
 
 
 def pack_kernel(first, flip, seconds, firsts, given, place_ref, ensemble_ref, *refs):
@@ -150,11 +149,16 @@
         lax.fori_loop(0, seconds, second, 0)
 
 
-def turn_kernel(firsts, seconds, taken, given, *refs):
-    sources, outs = views(refs[:taken], firsts), views(refs[-given:], seconds)
-    for g, out in enumerate(outs):
-        for patch in range(out.shape[0]):
-            out[patch] = jnp.concatenate([source[g, patch] for source in sources], axis=0)
+def turn_kernel(first, firsts, seconds, groups, taken, given, *refs):
+    outs = views(refs[-given:], seconds)
+    at = 0
+    for group in range(groups):
+        sources = views(refs[group * taken : (group + 1) * taken], firsts)
+        count = min(sources[0].shape[1] - first, outs[0].shape[0])
+        for g, out in enumerate(outs):
+            for patch in range(count):
+                out[at + patch] = jnp.concatenate([source[g, first + patch] for source in sources], axis=0)
+        at += count
 
 
 def unpack_kernel(flips, regions, partners, place_ref, *refs):
@@ -196,11 +200,10 @@
     held = obs_site.shape[0]
     place = lax.axis_index("member").astype(jnp.int32)[None]
     total = members * partners * regions
-    flips = [False, True]
-    counts = [held // 2, held - held // 2]
-    starts = [0, held // 2]
-    axes = [("member", "region"), ("region", "member")]
-    sizes = [(partners, regions), (regions, partners)]
+    y_count = held // 2
+    x_counts = [(held - y_count) // 2, held - y_count - (held - y_count) // 2]
+    x_count = sum(x_counts)
+    sizes = {"member": partners, "region": regions}
     last = [[]]
     state = {}
 
@@ -229,51 +232,55 @@
             [obs_site, obs_precision, obs_innovation],
         )
 
-    def pack(c):
-        first, second = sizes[c]
-        shapes = blocks(axes[c][0], first, second, counts[c], members)
+    def pack(c, first, count, axis, other):
+        shapes = blocks(axis, sizes[axis], sizes[other], count, members)
         packed = run(
-            functools.partial(pack_kernel, starts[c], flips[c], second, first, len(shapes)), "pack",
-            shapes, [place], [ensemble],
+            functools.partial(pack_kernel, first, axis == "region", sizes[other], sizes[axis], len(shapes)),
+            "pack", shapes, [place], [ensemble],
         )
-        state[c] = exchange(packed, axes[c][0])
-
-    def turn(c, flops=0):
-        first, second = sizes[c]
-        shapes = blocks(axes[c][1], second, counts[c], first * members)
+        state[c] = exchange(packed, axis)
+
+    def turn(c, sources, first, count, axis, other, flops=0):
+        arrays = [array for source in sources for array in state[source]]
+        shapes = blocks(other, sizes[other], count, sizes[axis] * members)
         turned = run(
-            functools.partial(turn_kernel, first, second, len(state[c]), len(shapes)), "turn",
-            shapes, [], state[c], flops,
+            functools.partial(
+                turn_kernel, first, sizes[axis], sizes[other], len(sources),
+                len(arrays) // len(sources), len(shapes),
+            ),
+            "turn", shapes, [], arrays, flops,
         )
-        state[c] = exchange(turned, axes[c][1])
-
-    def analyse(c):
-        first, second = sizes[c]
-        shapes = blocks(axes[c][0], first, second, counts[c], members)
+        state[c] = exchange(turned, other)
+
+    def analyse(c, first, count, axis, other, flops=0):
+        shapes = blocks(axis, sizes[axis], sizes[other], count, members)
         analysed = run(
-            functools.partial(analyse_kernel, starts[c], second, first, len(state[c]), len(shapes)), "analyse",
-            shapes, [], list(state["sums"]) + state[c],
-            0,
+            functools.partial(analyse_kernel, first, sizes[axis], len(shapes)), "analyse",
+            shapes, [], list(state["sums"]) + state[c], flops,
         )
-        state[c] = exchange(analysed, axes[c][0])
-
-    def hold(c, flops):
-        last[0] = last[0] + state[c]
+        state[c] = exchange(analysed, axis)
+
+    def hold(arrays, flops):
+        last[0] = last[0] + list(arrays)
         run(hold_kernel, "hold", [jax.ShapeDtypeStruct((8, LANES), F32)], [], [], flops)
 
-    pack(0)
-    pack(1)
+    pack("y", 0, y_count, "member", "region")
+    pack("x", y_count, x_count, "region", "member")
     site_sums()
-    turn(0, LONG)
-    turn(1)
-    analyse(0)
-    analyse(1)
-    turn(0, LONG)
-    turn(1)
-    hold(1, LONG)
+    hold(state["y"][1:-1], LONG)
+    turn("x0", ["x"], 0, x_counts[0], "region", "member")
+    turn("y", ["y"], 0, y_count, "member", "region", LONG)
+    turn("x1", ["x"], x_counts[0], x_counts[1], "region", "member")
+    analyse("x0", y_count, x_counts[0], "member", "region", LONG)
+    analyse("y", 0, y_count, "region", "member")
+    analyse("x1", y_count + x_counts[0], x_counts[1], "member", "region")
+    hold(state["x0"], SHORT)
+    turn("y", ["y"], 0, y_count, "region", "member")
+    turn("x", ["x0", "x1"], 0, x_count, "member", "region", LONG)
+    hold(state["y"], LONG)
     return run(
-        functools.partial(unpack_kernel, flips, regions, partners), "unpack",
-        [jax.ShapeDtypeStruct(ensemble.shape, BF16)], [place], state[0] + state[1],
+        functools.partial(unpack_kernel, [True, False], regions, partners), "unpack",
+        [jax.ShapeDtypeStruct(ensemble.shape, BF16)], [place], state["y"] + state["x"],
     )[0]
 
 

time: 119 us -> 116 us (0.975)
  waiting for transfers between devices: 50.4 us -> 34 us
  starting transfers between devices: 36.2 us -> 43.4 us
  Pallas kernels: 30.4 us -> 34.2 us
  local copies, waits for them, and re-layouts: 1.61 us -> 3.17 us
    all_to_all x4, waiting for transfers between devices: 23.8 us -> 10.4 us  [exchange(): lax.all_to_all(blocks[0], axis, split_axis=0, concat_axis=0, tiled=True)]
    ppermute x12 -> x18, starting transfers between devices: 21.6 us -> 27.7 us  [exchange(): lax.ppermute(blocks[k], axis, [(i, i ^ k) for i in range(size)])]
    pallas_call x11 -> x15, Pallas kernels: 30.4 us -> 34.2 us  [run(): pl.pallas_call(kernel, out_shape=shapes, in_specs=[SMEM] * len(scalars) +...]
    ppermute x12 -> x18, waiting for transfers between devices: 26.6 us -> 23.6 us  [exchange(): lax.ppermute(blocks[k], axis, [(i, i ^ k) for i in range(size)])]
    unnamed x10 -> x14, local copies, waits for them, and re-layouts: 1.61 us -> 3.17 us
  transfers between devices with their start and end apart: 16 -> 22, of which waited for: 9 -> 6; matrix products, arithmetic and copies ran while one was open for 0% -> 0% of each run, Pallas kernels for 23% -> 27%
where the time goes in v3:
time: 116 us; the launch traced here: 115 us
  starting transfers between devices  43.4 us (37%)
  Pallas kernels  34.2 us (29%)
  waiting for transfers between devices  34 us (29%)
  local copies, waits for them, and re-layouts  3.17 us (3%)
    pallas_call x15, Pallas kernels, run(): pl.pallas_call(kernel, out_shape=shapes, in_specs=[SMEM] * len(scalars) +...  34.2 us
    ppermute x18, starting transfers between devices, exchange(): lax.ppermute(blocks[k], axis, [(i, i ^ k) for i in range(size)])  27.7 us
    ppermute x18, waiting for transfers between devices, exchange(): lax.ppermute(blocks[k], axis, [(i, i ^ k) for i in range(size)])  23.6 us
    all_to_all x4, starting transfers between devices, exchange(): lax.all_to_all(blocks[0], axis, split_axis=0, concat_axis=0, tiled=True)  15.7 us
    all_to_all x4, waiting for transfers between devices, exchange(): lax.all_to_all(blocks[0], axis, split_axis=0, concat_axis=0, tiled=True)  10.4 us
    unnamed x14, local copies, waits for them, and re-layouts  3.17 us
  transfers between devices with their start and end apart: 22, of which 6 were waited for; matrix products, arithmetic and copies ran while one was open for 0% of the time, Pallas kernels for 27%

profile of v3, /device:TPU:0, one launch (start us, length us, event | category | flops | bytes accessed | tf_op | source)
XLA Modules:
  0.0 114.8 jit_solution(10059614192082114650)
XLA Ops:
  0.0 1.6 %copy-done = bf16[8,256,512]{2,1,0:T(8,128)(2,1)S(1)} copy-done((bf16[8,256,512]{2,1,0:T(8,128)(2,1)S(1)}, bf16[8,256,512]{2,1,0:T(8,128)(2,1)}, u32[]{:S(2)}) %copy-start) | copy-done | bytes 2097176
  1.6 0.8 pack.2
  2.4 3.1 %collective-permute-start = (bf16[8,4,8,512]{3,2,1,0:T(8,128)(2,1)S(1)}, bf16[8,4,8,512]{3,2,1,0:T(8,128)(2,1)S(1)}, u32[]{:S(2)}, u32[]{:S(2)}) collective-permute-start(bf16[8,4,8,512]{3,2,1,0:T(8,128)(2,1)S(1)} %get-tuple-element.34), channel_id=1, source_target_pairs={{0,8},{8,0},{16,24},{24,16},{1,9},{9,1},{17,25},{25,17},{2,10},{10... | collective-permute-start | bytes 786440 | tf_op jit(solution)/shard_map/ppermute | solution.py:194
  5.5 2.6 %collective-permute-start.1 = (bf16[8,4,8,512]{3,2,1,0:T(8,128)(2,1)S(1)}, bf16[8,4,8,512]{3,2,1,0:T(8,128)(2,1)S(1)}, u32[]{:S(2)}, u32[]{:S(2)}) collective-permute-start(bf16[8,4,8,512]{3,2,1,0:T(8,128)(2,1)S(1)} %get-tuple-element.35), channel_id=1, source_target_pairs={{0,16},{8,24},{16,0},{24,8},{1,17},{9,25},{17,1},{25,9},{2,18},{10... | collective-permute-start | bytes 786440 | tf_op jit(solution)/shard_map/ppermute | solution.py:194
  8.1 1.8 %pack.3.refs_0_ = bf16[8,4,4,8,512]{4,3,2,1,0:T(8,128)(2,1)} custom-call(s32[1]{0:T(128)} %bitcast.place_ref, bf16[8,256,512]{2,1,0:T(8,128)(2,1)S(1)} %copy-done, bf16[8,4,8,512]{3,2,1,0:T(8,128)(2,1)S(1)} %get-tuple-element.31.refs_0_), custom_call_target="tpu_custom_call" | custom-call | tf_op jit(solution)/shard_map/pack/pallas_call | solution.py:211
  9.9 3.9 %all-to-all-start = ((bf16[8,4,4,8,512]{4,3,2,1,0:T(8,128)(2,1)}), bf16[8,4,4,8,512]{4,3,2,1,0:T(8,128)(2,1)S(1)}, u32[]{:S(2)}, u32[]{:S(2)}) async-start(bf16[8,4,4,8,512]{4,3,2,1,0:T(8,128)(2,1)} %pack.3.refs_0_), calls=%async_computation | async-start | bytes 2097152 | tf_op jit(solution)/shard_map/all_to_all | solution.py:191
  13.9 1.7 %site_sums.1 = (f32[8,512]{1,0:T(8,128)S(1)}, f32[8,512]{1,0:T(8,128)S(1)}) custom-call(s32[8]{0:T(128)S(1)} %copy-done.4, s32[8,2048]{1,0:T(8,128)S(1)} %copy-done.1, bf16[8,2048]{1,0:T(8,128)(2,1)S(1)} %copy-done.2, bf16[8,2048]{1,0:T(8,128)(2,1)S(1)} %copy-done.3, bf16[8,4,4,8,512]{4,3,2,1,0:T(8,128)(2,1)} %pack.3.refs_0_), custom_call_target="tpu_custom_call" | custom-call | tf_op jit(solution)/shard_map/site_sums/pallas_call | solution.py:211
  15.6 1.0 collective-permute-done.refs_1_
  16.7 10.2 %collective-permute-done.1.refs_2_ = bf16[8,4,8,512]{3,2,1,0:T(8,128)(2,1)S(1)} collective-permute-done((bf16[8,4,8,512]{3,2,1,0:T(8,128)(2,1)S(1)}, bf16[8,4,8,512]{3,2,1,0:T(8,128)(2,1)S(1)}, u32[]{:S(2)}, u32[]{:S(2)}) %collective-permute-start.1) | collective-permute-done | bytes 262176 | tf_op jit(solution)/shard_map/ppermute | solution.py:194
  26.9 2.4 %all-to-all-done.refs_0_ = bf16[8,4,4,8,512]{4,3,2,1,0:T(8,128)(2,1)S(1)} async-done(((bf16[8,4,4,8,512]{4,3,2,1,0:T(8,128)(2,1)}), bf16[8,4,4,8,512]{4,3,2,1,0:T(8,128)(2,1)S(1)}, u32[]{:S(2)}, u32[]{:S(2)}) %all-to-all-start) | async-done | bytes 1048608 | tf_op jit(solution)/shard_map/all_to_all | solution.py:191
  29.3 0.7 turn.5
  29.9 0.7 collective-permute-start.3
  30.6 3.5 %collective-permute-start.4 = (bf16[2,64,512]{2,1,0:T(8,128)(2,1)}, bf16[2,64,512]{2,1,0:T(8,128)(2,1)S(1)}, u32[]{:S(2)}, u32[]{:S(2)}) collective-permute-start(bf16[2,64,512]{2,1,0:T(8,128)(2,1)} %get-tuple-element.39), channel_id=1, source_target_pairs={{0,16},{8,24},{16,0},{24,8},{1,17},{9,25},{17,1},{25,9},{2,18},{10... | collective-permute-start | bytes 393224 | tf_op jit(solution)/shard_map/ppermute | solution.py:194
  34.3 1.1 turn.6.refs_1_
  35.5 3.7 %all-to-all-start.1 = ((bf16[8,4,32,512]{3,2,1,0:T(8,128)(2,1)}), bf16[8,4,32,512]{3,2,1,0:T(8,128)(2,1)S(1)}, u32[]{:S(2)}, u32[]{:S(2)}) async-start(bf16[8,4,32,512]{3,2,1,0:T(8,128)(2,1)} %turn.6.refs_1_), calls=%async_computation.1 | async-start | bytes 2097152 | tf_op jit(solution)/shard_map/all_to_all | solution.py:191
  39.2 0.7 turn.7
  40.2 3.8 %collective-permute-start.7 = (bf16[2,64,512]{2,1,0:T(8,128)(2,1)}, bf16[2,64,512]{2,1,0:T(8,128)(2,1)S(1)}, u32[]{:S(2)}, u32[]{:S(2)}) collective-permute-start(bf16[2,64,512]{2,1,0:T(8,128)(2,1)} %get-tuple-element.44), channel_id=1, source_target_pairs={{0,16},{8,24},{16,0},{24,8},{1,17},{9,25},{17,1},{25,9},{2,18},{10... | collective-permute-start | bytes 393224 | tf_op jit(solution)/shard_map/ppermute | solution.py:194
  44.3 7.0 %analyse.3 = (bf16[8,2,8,512]{3,2,1,0:T(8,128)(2,1)S(1)}, bf16[8,2,8,512]{3,2,1,0:T(8,128)(2,1)}, bf16[8,2,8,512]{3,2,1,0:T(8,128)(2,1)}, bf16[8,2,8,512]{3,2,1,0:T(8,128)(2,1)S(1)}) custom-call(f32[8,512]{1,0:T(8,128)S(1)} %get-tuple-element.32.refs_0_.weight_ref, f32[8,512]{1,0:T(8,128)S(1)} %get-tuple-element.33.value_ref, ...), custom_call_target="tpu_custom_call" | custom-call | flops 99999997952 | tf_op jit(solution)/shard_map/analyse/pallas_call | solution.py:211
  51.6 3.8 %collective-permute-start.10 = (bf16[8,2,8,512]{3,2,1,0:T(8,128)(2,1)}, bf16[8,2,8,512]{3,2,1,0:T(8,128)(2,1)S(1)}, u32[]{:S(2)}, u32[]{:S(2)}) collective-permute-start(bf16[8,2,8,512]{3,2,1,0:T(8,128)(2,1)} %get-tuple-element.48), channel_id=1, source_target_pairs={{0,16},{8,24},{16,0},{24,8},{1,17},{9,25},{17,1},{25,9},{2,18},{10... | collective-permute-start | bytes 393224 | tf_op jit(solution)/shard_map/ppermute | solution.py:194
  55.7 9.8 %analyse.4.refs_4_ = bf16[8,4,4,8,512]{4,3,2,1,0:T(8,128)(2,1)} custom-call(f32[8,512]{1,0:T(8,128)S(1)} %get-tuple-element.32.refs_0_.weight_ref, f32[8,512]{1,0:T(8,128)S(1)} %get-tuple-element.33.value_ref, bf16[8,4,32,512]{3,2,1,0:T(8,128)(2,1)S(1)} %all-to-all-done.1.refs_0_, bf16[8,2,8,512]{3,2,1,0:T(8,128)(2,1)S(1)} %get-tuple-element.42.refs_1_.refs_0_), custom_call_target="tpu_custom_call" | custom-call | tf_op jit(solution)/shard_map/analyse/pallas_call | solution.py:211
  65.4 3.9 %all-to-all-start.2 = ((bf16[8,4,4,8,512]{4,3,2,1,0:T(8,128)(2,1)}), bf16[8,4,4,8,512]{4,3,2,1,0:T(8,128)(2,1)S(1)}, u32[]{:S(2)}, u32[]{:S(2)}) async-start(bf16[8,4,4,8,512]{4,3,2,1,0:T(8,128)(2,1)} %analyse.4.refs_4_), calls=%async_computation.2 | async-start | bytes 2097152 | tf_op jit(solution)/shard_map/all_to_all | solution.py:191
  69.4 6.0 %analyse.5 = (bf16[8,2,8,512]{3,2,1,0:T(8,128)(2,1)S(1)}, bf16[8,2,8,512]{3,2,1,0:T(8,128)(2,1)S(1)}, bf16[8,2,8,512]{3,2,1,0:T(8,128)(2,1)}, bf16[8,2,8,512]{3,2,1,0:T(8,128)(2,1)}) custom-call(f32[8,512]{1,0:T(8,128)S(1)} %get-tuple-element.32.refs_0_.weight_ref, f32[8,512]{1,0:T(8,128)S(1)} %get-tuple-element.33.value_ref, ...), custom_call_target="tpu_custom_call" | custom-call | tf_op jit(solution)/shard_map/analyse/pallas_call | solution.py:211
  75.8 3.8 %collective-permute-start.16 = (bf16[8,2,8,512]{3,2,1,0:T(8,128)(2,1)}, bf16[8,2,8,512]{3,2,1,0:T(8,128)(2,1)}, u32[]{:S(2)}, u32[]{:S(2)}) collective-permute-start(bf16[8,2,8,512]{3,2,1,0:T(8,128)(2,1)} %get-tuple-element.55), channel_id=1, source_target_pairs={{0,16},{8,24},{16,0},{24,8},{1,17},{9,25},{17,1},{25,9},{2,18},{10... | collective-permute-start | bytes 393224 | tf_op jit(solution)/shard_map/ppermute | solution.py:194
  79.8 5.0 %all-to-all-done.2.refs_0_ = bf16[8,4,4,8,512]{4,3,2,1,0:T(8,128)(2,1)S(1)} async-done(((bf16[8,4,4,8,512]{4,3,2,1,0:T(8,128)(2,1)}), bf16[8,4,4,8,512]{4,3,2,1,0:T(8,128)(2,1)S(1)}, u32[]{:S(2)}, u32[]{:S(2)}) %all-to-all-start.2) | async-done | bytes 1048608 | tf_op jit(solution)/shard_map/all_to_all | solution.py:191
  85.4 3.8 %collective-permute-start.13 = (bf16[4,64,512]{2,1,0:T(8,128)(2,1)S(1)}, bf16[4,64,512]{2,1,0:T(8,128)(2,1)S(1)}, u32[]{:S(2)}, u32[]{:S(2)}) collective-permute-start(bf16[4,64,512]{2,1,0:T(8,128)(2,1)S(1)} %get-tuple-element.52), channel_id=1, source_target_pairs={{0,16},{8,24},{16,0},{24,8},{1,17},{9,25},{17,1},{25,9},{2,18},{10... | collective-permute-start | bytes 786440 | tf_op jit(solution)/shard_map/ppermute | solution.py:194
  89.2 0.7 copy-done.5
  90.1 0.9 copy-done.6
  91.0 2.1 %turn.9.refs_0_ = bf16[8,4,32,512]{3,2,1,0:T(8,128)(2,1)} custom-call(bf16[8,2,8,512]{3,2,1,0:T(8,128)(2,1)S(1)} %get-tuple-element.42.refs_1_.refs_0_, bf16[8,2,8,512]{3,2,1,0:T(8,128)(2,1)S(1)} %collective-permute-done.9.refs_2_.refs_1_, bf16[8,2,8,512]{3,2,1,0:T(8,128)(2,1)S(1)} %collective-permute-done.10.refs_3_.refs_2_, ...), custom_call_target="tpu_custom_call" | custom-call | flops 99999997952 | tf_op jit(solution)/shard_map/turn/pallas_call | solution.py:211
  93.1 4.1 %all-to-all-start.3 = ((bf16[8,4,32,512]{3,2,1,0:T(8,128)(2,1)}), bf16[8,4,32,512]{3,2,1,0:T(8,128)(2,1)S(1)}, u32[]{:S(2)}, u32[]{:S(2)}) async-start(bf16[8,4,32,512]{3,2,1,0:T(8,128)(2,1)} %turn.9.refs_0_), calls=%async_computation.3 | async-start | bytes 2097152 | tf_op jit(solution)/shard_map/all_to_all | solution.py:191
  97.1 12.3 %collective-permute-done.13.refs_3_.refs_2_ = bf16[4,64,512]{2,1,0:T(8,128)(2,1)S(1)} collective-permute-done((bf16[4,64,512]{2,1,0:T(8,128)(2,1)S(1)}, bf16[4,64,512]{2,1,0:T(8,128)(2,1)S(1)}, u32[]{:S(2)}, u32[]{:S(2)}) %collective-permute-start.13) | collective-permute-done | bytes 262176 | tf_op jit(solution)/shard_map/ppermute | solution.py:194
  109.5 3.1 %all-to-all-done.3.refs_4_ = bf16[8,4,32,512]{3,2,1,0:T(8,128)(2,1)S(1)} async-done(((bf16[8,4,32,512]{3,2,1,0:T(8,128)(2,1)}), bf16[8,4,32,512]{3,2,1,0:T(8,128)(2,1)S(1)}, u32[]{:S(2)}, u32[]{:S(2)}) %all-to-all-start.3) | async-done | bytes 1048608 | tf_op jit(solution)/shard_map/all_to_all | solution.py:191
  112.5 2.3 %unpack.1 = bf16[8,256,512]{2,1,0:T(8,128)(2,1)} custom-call(s32[1]{0:T(128)} %bitcast.place_ref, bf16[4,64,512]{2,1,0:T(8,128)(2,1)S(1)} %get-tuple-element.50.refs_8_.refs_1_.refs_0_, bf16[4,64,512]{2,1,0:T(8,128)(2,1)S(1)} %collective-permute-done.12.refs_2_.refs_1_, bf16[4,64,512]{2,1,0:T(8,128)(2,1)S(1)} %collective-permute-done.13.refs_3_.refs_2_, ...), custom_call_target="tpu_custom_call" | custom-call | tf_op jit(solution)/shard_map/unpack/pallas_call | solution.py:211
  (41 shorter events, 2.8 us)
Async XLA Ops:
  0.0 1.6 %copy-start = (bf16[8,256,512]{2,1,0:T(8,128)(2,1)S(1)}, bf16[8,256,512]{2,1,0:T(8,128)(2,1)}, u32[]{:S(2)}) copy-start(bf16[8,256,512]{2,1,0:T(8,128)(2,1)} %ensemble_ref.3) | copy-start | bytes 6291460
  2.4 14.2 %collective-permute-start = (bf16[8,4,8,512]{3,2,1,0:T(8,128)(2,1)S(1)}, bf16[8,4,8,512]{3,2,1,0:T(8,128)(2,1)S(1)}, u32[]{:S(2)}, u32[]{:S(2)}) collective-permute-start(bf16[8,4,8,512]{3,2,1,0:T(8,128)(2,1)S(1)} %get-tuple-element.34), channel_id=1, source_target_pairs={{0,8},{8,0},{16,24},{24,16},{1,9},{9,1},{17,25},{25,17},{2,10},{10... | collective-permute-start | bytes 786440 | tf_op jit(solution)/shard_map/ppermute | solution.py:194
  5.5 21.4 %collective-permute-start.1 = (bf16[8,4,8,512]{3,2,1,0:T(8,128)(2,1)S(1)}, bf16[8,4,8,512]{3,2,1,0:T(8,128)(2,1)S(1)}, u32[]{:S(2)}, u32[]{:S(2)}) collective-permute-start(bf16[8,4,8,512]{3,2,1,0:T(8,128)(2,1)S(1)} %get-tuple-element.35), channel_id=1, source_target_pairs={{0,16},{8,24},{16,0},{24,8},{1,17},{9,25},{17,1},{25,9},{2,18},{10... | collective-permute-start | bytes 786440 | tf_op jit(solution)/shard_map/ppermute | solution.py:194
  8.1 26.2 %collective-permute-start.2 = (bf16[8,4,8,512]{3,2,1,0:T(8,128)(2,1)S(1)}, bf16[8,4,8,512]{3,2,1,0:T(8,128)(2,1)S(1)}, u32[]{:S(2)}, u32[]{:S(2)}) collective-permute-start(bf16[8,4,8,512]{3,2,1,0:T(8,128)(2,1)S(1)} %get-tuple-element.36), channel_id=1, source_target_pairs={{0,24},{8,16},{16,8},{24,0},{1,25},{9,17},{17,9},{25,1},{2,26},{10... | collective-permute-start | bytes 786440 | tf_op jit(solution)/shard_map/ppermute | solution.py:194
  8.1 5.8 %copy-start.1 = (s32[8,2048]{1,0:T(8,128)S(1)}, s32[8,2048]{1,0:T(8,128)}, u32[]{:S(2)}) copy-start(s32[8,2048]{1,0:T(8,128)} %site_ref.1) | copy-start | bytes 196612
  8.1 5.8 %copy-start.2 = (bf16[8,2048]{1,0:T(8,128)(2,1)S(1)}, bf16[8,2048]{1,0:T(8,128)(2,1)}, u32[]{:S(2)}) copy-start(bf16[8,2048]{1,0:T(8,128)(2,1)} %precision_ref.1) | copy-start | bytes 98308
  8.1 5.8 %copy-start.3 = (bf16[8,2048]{1,0:T(8,128)(2,1)S(1)}, bf16[8,2048]{1,0:T(8,128)(2,1)}, u32[]{:S(2)}) copy-start(bf16[8,2048]{1,0:T(8,128)(2,1)} %innovation_ref.1) | copy-start | bytes 98308
  8.1 5.8 %copy-start.4 = (s32[8]{0:T(128)S(1)}, s32[8]{0:T(128)}, u32[]{:S(2)}) copy-start(s32[8]{0:T(128)} %blocks_ref.1) | copy-start | bytes 100
  9.9 19.3 %all-to-all-start = ((bf16[8,4,4,8,512]{4,3,2,1,0:T(8,128)(2,1)}), bf16[8,4,4,8,512]{4,3,2,1,0:T(8,128)(2,1)S(1)}, u32[]{:S(2)}, u32[]{:S(2)}) async-start(bf16[8,4,4,8,512]{4,3,2,1,0:T(8,128)(2,1)} %pack.3.refs_0_), calls=%async_computation | async-start | bytes 2097152 | tf_op jit(solution)/shard_map/all_to_all | solution.py:191
  29.9 14.1 %collective-permute-start.3 = (bf16[2,64,512]{2,1,0:T(8,128)(2,1)S(1)}, bf16[2,64,512]{2,1,0:T(8,128)(2,1)S(1)}, u32[]{:S(2)}, u32[]{:S(2)}) collective-permute-start(bf16[2,64,512]{2,1,0:T(8,128)(2,1)S(1)} %get-tuple-element.38), channel_id=1, source_target_pairs={{0,8},{8,0},{16,24},{24,16},{1,9},{9,1},{17,25},{25,17},{2,10},{10... | collective-permute-start | bytes 393224 | tf_op jit(solution)/shard_map/ppermute | solution.py:194
  30.6 13.7 %collective-permute-start.4 = (bf16[2,64,512]{2,1,0:T(8,128)(2,1)}, bf16[2,64,512]{2,1,0:T(8,128)(2,1)S(1)}, u32[]{:S(2)}, u32[]{:S(2)}) collective-permute-start(bf16[2,64,512]{2,1,0:T(8,128)(2,1)} %get-tuple-element.39), channel_id=1, source_target_pairs={{0,16},{8,24},{16,0},{24,8},{1,17},{9,25},{17,1},{25,9},{2,18},{10... | collective-permute-start | bytes 393224 | tf_op jit(solution)/shard_map/ppermute | solution.py:194
  34.1 10.2 %collective-permute-start.5 = (bf16[2,64,512]{2,1,0:T(8,128)(2,1)S(1)}, bf16[2,64,512]{2,1,0:T(8,128)(2,1)}, u32[]{:S(2)}, u32[]{:S(2)}) collective-permute-start(bf16[2,64,512]{2,1,0:T(8,128)(2,1)S(1)} %get-tuple-element.40), channel_id=1, source_target_pairs={{0,24},{8,16},{16,8},{24,0},{1,25},{9,17},{17,9},{25,1},{2,26},{10... | collective-permute-start | bytes 393224 | tf_op jit(solution)/shard_map/ppermute | solution.py:194
  35.5 20.2 %all-to-all-start.1 = ((bf16[8,4,32,512]{3,2,1,0:T(8,128)(2,1)}), bf16[8,4,32,512]{3,2,1,0:T(8,128)(2,1)S(1)}, u32[]{:S(2)}, u32[]{:S(2)}) async-start(bf16[8,4,32,512]{3,2,1,0:T(8,128)(2,1)} %turn.6.refs_1_), calls=%async_computation.1 | async-start | bytes 2097152 | tf_op jit(solution)/shard_map/all_to_all | solution.py:191
  39.9 15.5 %collective-permute-start.6 = (bf16[2,64,512]{2,1,0:T(8,128)(2,1)S(1)}, bf16[2,64,512]{2,1,0:T(8,128)(2,1)S(1)}, u32[]{:S(2)}, u32[]{:S(2)}) collective-permute-start(bf16[2,64,512]{2,1,0:T(8,128)(2,1)S(1)} %get-tuple-element.43), channel_id=1, source_target_pairs={{0,8},{8,0},{16,24},{24,16},{1,9},{9,1},{17,25},{25,17},{2,10},{10... | collective-permute-start | bytes 393224 | tf_op jit(solution)/shard_map/ppermute | solution.py:194
  40.2 29.2 %collective-permute-start.7 = (bf16[2,64,512]{2,1,0:T(8,128)(2,1)}, bf16[2,64,512]{2,1,0:T(8,128)(2,1)S(1)}, u32[]{:S(2)}, u32[]{:S(2)}) collective-permute-start(bf16[2,64,512]{2,1,0:T(8,128)(2,1)} %get-tuple-element.44), channel_id=1, source_target_pairs={{0,16},{8,24},{16,0},{24,8},{1,17},{9,25},{17,1},{25,9},{2,18},{10... | collective-permute-start | bytes 393224 | tf_op jit(solution)/shard_map/ppermute | solution.py:194
  44.1 25.3 %collective-permute-start.8 = (bf16[2,64,512]{2,1,0:T(8,128)(2,1)S(1)}, bf16[2,64,512]{2,1,0:T(8,128)(2,1)S(1)}, u32[]{:S(2)}, u32[]{:S(2)}) collective-permute-start(bf16[2,64,512]{2,1,0:T(8,128)(2,1)S(1)} %get-tuple-element.45), channel_id=1, source_target_pairs={{0,24},{8,16},{16,8},{24,0},{1,25},{9,17},{17,9},{25,1},{2,26},{10... | collective-permute-start | bytes 393224 | tf_op jit(solution)/shard_map/ppermute | solution.py:194
  51.3 28.3 %collective-permute-start.9 = (bf16[8,2,8,512]{3,2,1,0:T(8,128)(2,1)}, bf16[8,2,8,512]{3,2,1,0:T(8,128)(2,1)S(1)}, u32[]{:S(2)}, u32[]{:S(2)}) collective-permute-start(bf16[8,2,8,512]{3,2,1,0:T(8,128)(2,1)} %get-tuple-element.47), channel_id=1, source_target_pairs={{0,8},{8,0},{16,24},{24,16},{1,9},{9,1},{17,25},{25,17},{2,10},{10... | collective-permute-start | bytes 393224 | tf_op jit(solution)/shard_map/ppermute | solution.py:194
  51.6 28.2 %collective-permute-start.10 = (bf16[8,2,8,512]{3,2,1,0:T(8,128)(2,1)}, bf16[8,2,8,512]{3,2,1,0:T(8,128)(2,1)S(1)}, u32[]{:S(2)}, u32[]{:S(2)}) collective-permute-start(bf16[8,2,8,512]{3,2,1,0:T(8,128)(2,1)} %get-tuple-element.48), channel_id=1, source_target_pairs={{0,16},{8,24},{16,0},{24,8},{1,17},{9,25},{17,1},{25,9},{2,18},{10... | collective-permute-start | bytes 393224 | tf_op jit(solution)/shard_map/ppermute | solution.py:194
  55.4 24.4 %collective-permute-start.11 = (bf16[8,2,8,512]{3,2,1,0:T(8,128)(2,1)S(1)}, bf16[8,2,8,512]{3,2,1,0:T(8,128)(2,1)S(1)}, u32[]{:S(2)}, u32[]{:S(2)}) collective-permute-start(bf16[8,2,8,512]{3,2,1,0:T(8,128)(2,1)S(1)} %get-tuple-element.49), channel_id=1, source_target_pairs={{0,24},{8,16},{16,8},{24,0},{1,25},{9,17},{17,9},{25,1},{2,26},{10... | collective-permute-start | bytes 393224 | tf_op jit(solution)/shard_map/ppermute | solution.py:194
  65.4 19.4 %all-to-all-start.2 = ((bf16[8,4,4,8,512]{4,3,2,1,0:T(8,128)(2,1)}), bf16[8,4,4,8,512]{4,3,2,1,0:T(8,128)(2,1)S(1)}, u32[]{:S(2)}, u32[]{:S(2)}) async-start(bf16[8,4,4,8,512]{4,3,2,1,0:T(8,128)(2,1)} %analyse.4.refs_4_), calls=%async_computation.2 | async-start | bytes 2097152 | tf_op jit(solution)/shard_map/all_to_all | solution.py:191
  75.4 13.7 %collective-permute-start.15 = (bf16[8,2,8,512]{3,2,1,0:T(8,128)(2,1)S(1)}, bf16[8,2,8,512]{3,2,1,0:T(8,128)(2,1)S(1)}, u32[]{:S(2)}, u32[]{:S(2)}) collective-permute-start(bf16[8,2,8,512]{3,2,1,0:T(8,128)(2,1)S(1)} %get-tuple-element.54), channel_id=1, source_target_pairs={{0,8},{8,0},{16,24},{24,16},{1,9},{9,1},{17,25},{25,17},{2,10},{10... | collective-permute-start | bytes 393224 | tf_op jit(solution)/shard_map/ppermute | solution.py:194
  75.8 14.3 %collective-permute-start.16 = (bf16[8,2,8,512]{3,2,1,0:T(8,128)(2,1)}, bf16[8,2,8,512]{3,2,1,0:T(8,128)(2,1)}, u32[]{:S(2)}, u32[]{:S(2)}) collective-permute-start(bf16[8,2,8,512]{3,2,1,0:T(8,128)(2,1)} %get-tuple-element.55), channel_id=1, source_target_pairs={{0,16},{8,24},{16,0},{24,8},{1,17},{9,25},{17,1},{25,9},{2,18},{10... | collective-permute-start | bytes 393224 | tf_op jit(solution)/shard_map/ppermute | solution.py:194
  79.6 10.5 %collective-permute-start.17 = (bf16[8,2,8,512]{3,2,1,0:T(8,128)(2,1)}, bf16[8,2,8,512]{3,2,1,0:T(8,128)(2,1)}, u32[]{:S(2)}, u32[]{:S(2)}) collective-permute-start(bf16[8,2,8,512]{3,2,1,0:T(8,128)(2,1)} %get-tuple-element.56), channel_id=1, source_target_pairs={{0,24},{8,16},{16,8},{24,0},{1,25},{9,17},{17,9},{25,1},{2,26},{10... | collective-permute-start | bytes 393224 | tf_op jit(solution)/shard_map/ppermute | solution.py:194
  85.0 12.2 %collective-permute-start.12 = (bf16[4,64,512]{2,1,0:T(8,128)(2,1)S(1)}, bf16[4,64,512]{2,1,0:T(8,128)(2,1)S(1)}, u32[]{:S(2)}, u32[]{:S(2)}) collective-permute-start(bf16[4,64,512]{2,1,0:T(8,128)(2,1)S(1)} %get-tuple-element.51), channel_id=1, source_target_pairs={{0,8},{8,0},{16,24},{24,16},{1,9},{9,1},{17,25},{25,17},{2,10},{10... | collective-permute-start | bytes 786440 | tf_op jit(solution)/shard_map/ppermute | solution.py:194
  85.4 24.1 %collective-permute-start.13 = (bf16[4,64,512]{2,1,0:T(8,128)(2,1)S(1)}, bf16[4,64,512]{2,1,0:T(8,128)(2,1)S(1)}, u32[]{:S(2)}, u32[]{:S(2)}) collective-permute-start(bf16[4,64,512]{2,1,0:T(8,128)(2,1)S(1)} %get-tuple-element.52), channel_id=1, source_target_pairs={{0,16},{8,24},{16,0},{24,8},{1,17},{9,25},{17,1},{25,9},{2,18},{10... | collective-permute-start | bytes 786440 | tf_op jit(solution)/shard_map/ppermute | solution.py:194
  89.2 0.7 copy-start.5
  89.8 19.6 %collective-permute-start.14 = (bf16[4,64,512]{2,1,0:T(8,128)(2,1)S(1)}, bf16[4,64,512]{2,1,0:T(8,128)(2,1)S(1)}, u32[]{:S(2)}, u32[]{:S(2)}) collective-permute-start(bf16[4,64,512]{2,1,0:T(8,128)(2,1)S(1)} %get-tuple-element.53), channel_id=1, source_target_pairs={{0,24},{8,16},{16,8},{24,0},{1,25},{9,17},{17,9},{25,1},{2,26},{10... | collective-permute-start | bytes 786440 | tf_op jit(solution)/shard_map/ppermute | solution.py:194
  90.1 0.9 copy-start.6
  93.1 19.5 %all-to-all-start.3 = ((bf16[8,4,32,512]{3,2,1,0:T(8,128)(2,1)}), bf16[8,4,32,512]{3,2,1,0:T(8,128)(2,1)S(1)}, u32[]{:S(2)}, u32[]{:S(2)}) async-start(bf16[8,4,32,512]{3,2,1,0:T(8,128)(2,1)} %turn.9.refs_0_), calls=%async_computation.3 | async-start | bytes 2097152 | tf_op jit(solution)/shard_map/all_to_all | solution.py:191

commit v4 on v3

--- a/solution.py
+++ b/solution.py
@@ -43,6 +43,14 @@
         jnp.concatenate([left[0], left[0], left[1]], axis=1),
         jnp.concatenate([right[0], right[1], right[0]], axis=0),
     )
+
+
+def dot_stacked(lefts, right):
+    rows = sum(left[0].shape[0] for left in lefts)
+    highs = [left[0] for left in lefts]
+    main = dot(jnp.concatenate(highs + [left[1] for left in lefts], axis=0), right[0])
+    rest = dot(jnp.concatenate(highs, axis=0), right[1]) if len(highs) > 1 else dot(highs[0], right[1])
+    return main[:rows] + (main[rows:] + rest)
 
 
 def site_sums_kernel(states, blocks_ref, site_ref, precision_ref, innovation_ref, *refs):
@@ -108,15 +116,18 @@
         rests.append(eye - amat * scale)
 
     zs = [eye + 0.5 * rest for rest in rests]
-    parts = [split(rest) for rest in rests]
     for step in range(1, ITERS):
-        squares = [dot_split(part_, part_) for part_ in parts]
-        halves = [split(0.25 * square) for square in squares]
+        parts = [split(rest) for rest in rests]
+        if step == 1:
+            squares = [dot_split(part_, part_) for part_ in parts]
+        else:
+            both = [dot_stacked([part_, split(z)], part_) for part_, z in zip(parts, zs)]
+            squares = [pair[:members] for pair in both]
+            zs = [z + 0.5 * pair[members:] for z, pair in zip(zs, both)]
         rests = [
-            0.75 * square + dot_split(half, part_) for square, half, part_ in zip(squares, halves, parts)
+            0.75 * square + dot_stacked([split(0.25 * square)], part_) for square, part_ in zip(squares, parts)
         ]
-        parts = [split(rest) for rest in rests]
-        zs = [z + 0.5 * dot_split(part_, split(z)) for part_, z in zip(parts, zs)]
+    zs = [z + 0.5 * dot_split(split(z), split(rest)) for rest, z in zip(rests, zs)]
 
     for patch in every:
         z = split(zs[patch])

time: 116 us -> 116 us (level)
  no operation moved by 1% of the time
where the time goes in v4:
time: 116 us; the launch traced here: 115 us
  starting transfers between devices  43.4 us (37%)
  Pallas kernels  34.2 us (29%)
  waiting for transfers between devices  34 us (29%)
  local copies, waits for them, and re-layouts  3.17 us (3%)
    pallas_call x15, Pallas kernels, run(): pl.pallas_call(kernel, out_shape=shapes, in_specs=[SMEM] * len(scalars) +...  34.2 us
    ppermute x18, starting transfers between devices, exchange(): lax.ppermute(blocks[k], axis, [(i, i ^ k) for i in range(size)])  27.7 us
    ppermute x18, waiting for transfers between devices, exchange(): lax.ppermute(blocks[k], axis, [(i, i ^ k) for i in range(size)])  23.6 us
    all_to_all x4, starting transfers between devices, exchange(): lax.all_to_all(blocks[0], axis, split_axis=0, concat_axis=0, tiled=True)  15.7 us
    all_to_all x4, waiting for transfers between devices, exchange(): lax.all_to_all(blocks[0], axis, split_axis=0, concat_axis=0, tiled=True)  10.4 us
    unnamed x14, local copies, waits for them, and re-layouts  3.17 us
  transfers between devices with their start and end apart: 22, of which 6 were waited for; matrix products, arithmetic and copies ran while one was open for 0% of the time, Pallas kernels for 27%

profile of v4, /device:TPU:0, one launch (start us, length us, event | category | flops | bytes accessed | tf_op | source)
XLA Modules:
  0.0 114.8 jit_solution(15601164332530091238)
XLA Ops:
  0.0 1.6 %copy-done = bf16[8,256,512]{2,1,0:T(8,128)(2,1)S(1)} copy-done((bf16[8,256,512]{2,1,0:T(8,128)(2,1)S(1)}, bf16[8,256,512]{2,1,0:T(8,128)(2,1)}, u32[]{:S(2)}) %copy-start) | copy-done | bytes 2097176
  1.6 0.8 pack.2
  2.4 3.1 %collective-permute-start = (bf16[8,4,8,512]{3,2,1,0:T(8,128)(2,1)S(1)}, bf16[8,4,8,512]{3,2,1,0:T(8,128)(2,1)S(1)}, u32[]{:S(2)}, u32[]{:S(2)}) collective-permute-start(bf16[8,4,8,512]{3,2,1,0:T(8,128)(2,1)S(1)} %get-tuple-element.34), channel_id=1, source_target_pairs={{0,8},{8,0},{16,24},{24,16},{1,9},{9,1},{17,25},{25,17},{2,10},{10... | collective-permute-start | bytes 786440 | tf_op jit(solution)/shard_map/ppermute | solution.py:205
  5.5 2.6 %collective-permute-start.1 = (bf16[8,4,8,512]{3,2,1,0:T(8,128)(2,1)S(1)}, bf16[8,4,8,512]{3,2,1,0:T(8,128)(2,1)S(1)}, u32[]{:S(2)}, u32[]{:S(2)}) collective-permute-start(bf16[8,4,8,512]{3,2,1,0:T(8,128)(2,1)S(1)} %get-tuple-element.35), channel_id=1, source_target_pairs={{0,16},{8,24},{16,0},{24,8},{1,17},{9,25},{17,1},{25,9},{2,18},{10... | collective-permute-start | bytes 786440 | tf_op jit(solution)/shard_map/ppermute | solution.py:205
  8.1 1.8 %pack.3.refs_0_ = bf16[8,4,4,8,512]{4,3,2,1,0:T(8,128)(2,1)} custom-call(s32[1]{0:T(128)} %bitcast.place_ref, bf16[8,256,512]{2,1,0:T(8,128)(2,1)S(1)} %copy-done, bf16[8,4,8,512]{3,2,1,0:T(8,128)(2,1)S(1)} %get-tuple-element.31.refs_0_), custom_call_target="tpu_custom_call" | custom-call | tf_op jit(solution)/shard_map/pack/pallas_call | solution.py:222
  9.9 3.9 %all-to-all-start = ((bf16[8,4,4,8,512]{4,3,2,1,0:T(8,128)(2,1)}), bf16[8,4,4,8,512]{4,3,2,1,0:T(8,128)(2,1)S(1)}, u32[]{:S(2)}, u32[]{:S(2)}) async-start(bf16[8,4,4,8,512]{4,3,2,1,0:T(8,128)(2,1)} %pack.3.refs_0_), calls=%async_computation | async-start | bytes 2097152 | tf_op jit(solution)/shard_map/all_to_all | solution.py:202
  13.9 1.7 %site_sums.1 = (f32[8,512]{1,0:T(8,128)S(1)}, f32[8,512]{1,0:T(8,128)S(1)}) custom-call(s32[8]{0:T(128)S(1)} %copy-done.4, s32[8,2048]{1,0:T(8,128)S(1)} %copy-done.1, bf16[8,2048]{1,0:T(8,128)(2,1)S(1)} %copy-done.2, bf16[8,2048]{1,0:T(8,128)(2,1)S(1)} %copy-done.3, bf16[8,4,4,8,512]{4,3,2,1,0:T(8,128)(2,1)} %pack.3.refs_0_), custom_call_target="tpu_custom_call" | custom-call | tf_op jit(solution)/shard_map/site_sums/pallas_call | solution.py:222
  15.6 1.0 collective-permute-done.refs_1_
  16.7 10.2 %collective-permute-done.1.refs_2_ = bf16[8,4,8,512]{3,2,1,0:T(8,128)(2,1)S(1)} collective-permute-done((bf16[8,4,8,512]{3,2,1,0:T(8,128)(2,1)S(1)}, bf16[8,4,8,512]{3,2,1,0:T(8,128)(2,1)S(1)}, u32[]{:S(2)}, u32[]{:S(2)}) %collective-permute-start.1) | collective-permute-done | bytes 262176 | tf_op jit(solution)/shard_map/ppermute | solution.py:205
  26.9 2.4 %all-to-all-done.refs_0_ = bf16[8,4,4,8,512]{4,3,2,1,0:T(8,128)(2,1)S(1)} async-done(((bf16[8,4,4,8,512]{4,3,2,1,0:T(8,128)(2,1)}), bf16[8,4,4,8,512]{4,3,2,1,0:T(8,128)(2,1)S(1)}, u32[]{:S(2)}, u32[]{:S(2)}) %all-to-all-start) | async-done | bytes 1048608 | tf_op jit(solution)/shard_map/all_to_all | solution.py:202
  29.3 0.7 turn.5
  29.9 0.7 collective-permute-start.3
  30.6 3.5 %collective-permute-start.4 = (bf16[2,64,512]{2,1,0:T(8,128)(2,1)}, bf16[2,64,512]{2,1,0:T(8,128)(2,1)S(1)}, u32[]{:S(2)}, u32[]{:S(2)}) collective-permute-start(bf16[2,64,512]{2,1,0:T(8,128)(2,1)} %get-tuple-element.39), channel_id=1, source_target_pairs={{0,16},{8,24},{16,0},{24,8},{1,17},{9,25},{17,1},{25,9},{2,18},{10... | collective-permute-start | bytes 393224 | tf_op jit(solution)/shard_map/ppermute | solution.py:205
  34.3 1.1 turn.6.refs_1_
  35.5 3.7 %all-to-all-start.1 = ((bf16[8,4,32,512]{3,2,1,0:T(8,128)(2,1)}), bf16[8,4,32,512]{3,2,1,0:T(8,128)(2,1)S(1)}, u32[]{:S(2)}, u32[]{:S(2)}) async-start(bf16[8,4,32,512]{3,2,1,0:T(8,128)(2,1)} %turn.6.refs_1_), calls=%async_computation.1 | async-start | bytes 2097152 | tf_op jit(solution)/shard_map/all_to_all | solution.py:202
  39.2 0.7 turn.7
  40.2 3.8 %collective-permute-start.7 = (bf16[2,64,512]{2,1,0:T(8,128)(2,1)}, bf16[2,64,512]{2,1,0:T(8,128)(2,1)S(1)}, u32[]{:S(2)}, u32[]{:S(2)}) collective-permute-start(bf16[2,64,512]{2,1,0:T(8,128)(2,1)} %get-tuple-element.44), channel_id=1, source_target_pairs={{0,16},{8,24},{16,0},{24,8},{1,17},{9,25},{17,1},{25,9},{2,18},{10... | collective-permute-start | bytes 393224 | tf_op jit(solution)/shard_map/ppermute | solution.py:205
  44.3 7.0 %analyse.3 = (bf16[8,2,8,512]{3,2,1,0:T(8,128)(2,1)S(1)}, bf16[8,2,8,512]{3,2,1,0:T(8,128)(2,1)}, bf16[8,2,8,512]{3,2,1,0:T(8,128)(2,1)}, bf16[8,2,8,512]{3,2,1,0:T(8,128)(2,1)S(1)}) custom-call(f32[8,512]{1,0:T(8,128)S(1)} %get-tuple-element.32.refs_0_.weight_ref, f32[8,512]{1,0:T(8,128)S(1)} %get-tuple-element.33.value_ref, ...), custom_call_target="tpu_custom_call" | custom-call | flops 99999997952 | tf_op jit(solution)/shard_map/analyse/pallas_call | solution.py:222
  51.6 3.8 %collective-permute-start.10 = (bf16[8,2,8,512]{3,2,1,0:T(8,128)(2,1)}, bf16[8,2,8,512]{3,2,1,0:T(8,128)(2,1)S(1)}, u32[]{:S(2)}, u32[]{:S(2)}) collective-permute-start(bf16[8,2,8,512]{3,2,1,0:T(8,128)(2,1)} %get-tuple-element.48), channel_id=1, source_target_pairs={{0,16},{8,24},{16,0},{24,8},{1,17},{9,25},{17,1},{25,9},{2,18},{10... | collective-permute-start | bytes 393224 | tf_op jit(solution)/shard_map/ppermute | solution.py:205
  55.7 9.7 %analyse.4.refs_4_ = bf16[8,4,4,8,512]{4,3,2,1,0:T(8,128)(2,1)} custom-call(f32[8,512]{1,0:T(8,128)S(1)} %get-tuple-element.32.refs_0_.weight_ref, f32[8,512]{1,0:T(8,128)S(1)} %get-tuple-element.33.value_ref, bf16[8,4,32,512]{3,2,1,0:T(8,128)(2,1)S(1)} %all-to-all-done.1.refs_0_, bf16[8,2,8,512]{3,2,1,0:T(8,128)(2,1)S(1)} %get-tuple-element.42.refs_1_.refs_0_), custom_call_target="tpu_custom_call" | custom-call | tf_op jit(solution)/shard_map/analyse/pallas_call | solution.py:222
  65.4 3.9 %all-to-all-start.2 = ((bf16[8,4,4,8,512]{4,3,2,1,0:T(8,128)(2,1)}), bf16[8,4,4,8,512]{4,3,2,1,0:T(8,128)(2,1)S(1)}, u32[]{:S(2)}, u32[]{:S(2)}) async-start(bf16[8,4,4,8,512]{4,3,2,1,0:T(8,128)(2,1)} %analyse.4.refs_4_), calls=%async_computation.2 | async-start | bytes 2097152 | tf_op jit(solution)/shard_map/all_to_all | solution.py:202
  69.3 6.1 %analyse.5 = (bf16[8,2,8,512]{3,2,1,0:T(8,128)(2,1)S(1)}, bf16[8,2,8,512]{3,2,1,0:T(8,128)(2,1)S(1)}, bf16[8,2,8,512]{3,2,1,0:T(8,128)(2,1)}, bf16[8,2,8,512]{3,2,1,0:T(8,128)(2,1)}) custom-call(f32[8,512]{1,0:T(8,128)S(1)} %get-tuple-element.32.refs_0_.weight_ref, f32[8,512]{1,0:T(8,128)S(1)} %get-tuple-element.33.value_ref, ...), custom_call_target="tpu_custom_call" | custom-call | tf_op jit(solution)/shard_map/analyse/pallas_call | solution.py:222
  75.8 3.8 %collective-permute-start.16 = (bf16[8,2,8,512]{3,2,1,0:T(8,128)(2,1)}, bf16[8,2,8,512]{3,2,1,0:T(8,128)(2,1)}, u32[]{:S(2)}, u32[]{:S(2)}) collective-permute-start(bf16[8,2,8,512]{3,2,1,0:T(8,128)(2,1)} %get-tuple-element.55), channel_id=1, source_target_pairs={{0,16},{8,24},{16,0},{24,8},{1,17},{9,25},{17,1},{25,9},{2,18},{10... | collective-permute-start | bytes 393224 | tf_op jit(solution)/shard_map/ppermute | solution.py:205
  79.9 4.9 %all-to-all-done.2.refs_0_ = bf16[8,4,4,8,512]{4,3,2,1,0:T(8,128)(2,1)S(1)} async-done(((bf16[8,4,4,8,512]{4,3,2,1,0:T(8,128)(2,1)}), bf16[8,4,4,8,512]{4,3,2,1,0:T(8,128)(2,1)S(1)}, u32[]{:S(2)}, u32[]{:S(2)}) %all-to-all-start.2) | async-done | bytes 1048608 | tf_op jit(solution)/shard_map/all_to_all | solution.py:202
  85.3 3.8 %collective-permute-start.13 = (bf16[4,64,512]{2,1,0:T(8,128)(2,1)S(1)}, bf16[4,64,512]{2,1,0:T(8,128)(2,1)S(1)}, u32[]{:S(2)}, u32[]{:S(2)}) collective-permute-start(bf16[4,64,512]{2,1,0:T(8,128)(2,1)S(1)} %get-tuple-element.52), channel_id=1, source_target_pairs={{0,16},{8,24},{16,0},{24,8},{1,17},{9,25},{17,1},{25,9},{2,18},{10... | collective-permute-start | bytes 786440 | tf_op jit(solution)/shard_map/ppermute | solution.py:205
  89.1 0.7 copy-done.5
  90.0 0.9 copy-done.6
  90.9 2.1 %turn.9.refs_0_ = bf16[8,4,32,512]{3,2,1,0:T(8,128)(2,1)} custom-call(bf16[8,2,8,512]{3,2,1,0:T(8,128)(2,1)S(1)} %get-tuple-element.42.refs_1_.refs_0_, bf16[8,2,8,512]{3,2,1,0:T(8,128)(2,1)S(1)} %collective-permute-done.9.refs_2_.refs_1_, bf16[8,2,8,512]{3,2,1,0:T(8,128)(2,1)S(1)} %collective-permute-done.10.refs_3_.refs_2_, ...), custom_call_target="tpu_custom_call" | custom-call | flops 99999997952 | tf_op jit(solution)/shard_map/turn/pallas_call | solution.py:222
  93.0 4.1 %all-to-all-start.3 = ((bf16[8,4,32,512]{3,2,1,0:T(8,128)(2,1)}), bf16[8,4,32,512]{3,2,1,0:T(8,128)(2,1)S(1)}, u32[]{:S(2)}, u32[]{:S(2)}) async-start(bf16[8,4,32,512]{3,2,1,0:T(8,128)(2,1)} %turn.9.refs_0_), calls=%async_computation.3 | async-start | bytes 2097152 | tf_op jit(solution)/shard_map/all_to_all | solution.py:202
  97.1 12.3 %collective-permute-done.13.refs_3_.refs_2_ = bf16[4,64,512]{2,1,0:T(8,128)(2,1)S(1)} collective-permute-done((bf16[4,64,512]{2,1,0:T(8,128)(2,1)S(1)}, bf16[4,64,512]{2,1,0:T(8,128)(2,1)S(1)}, u32[]{:S(2)}, u32[]{:S(2)}) %collective-permute-start.13) | collective-permute-done | bytes 262176 | tf_op jit(solution)/shard_map/ppermute | solution.py:205
  109.4 3.1 %all-to-all-done.3.refs_4_ = bf16[8,4,32,512]{3,2,1,0:T(8,128)(2,1)S(1)} async-done(((bf16[8,4,32,512]{3,2,1,0:T(8,128)(2,1)}), bf16[8,4,32,512]{3,2,1,0:T(8,128)(2,1)S(1)}, u32[]{:S(2)}, u32[]{:S(2)}) %all-to-all-start.3) | async-done | bytes 1048608 | tf_op jit(solution)/shard_map/all_to_all | solution.py:202
  112.5 2.3 %unpack.1 = bf16[8,256,512]{2,1,0:T(8,128)(2,1)} custom-call(s32[1]{0:T(128)} %bitcast.place_ref, bf16[4,64,512]{2,1,0:T(8,128)(2,1)S(1)} %get-tuple-element.50.refs_8_.refs_1_.refs_0_, bf16[4,64,512]{2,1,0:T(8,128)(2,1)S(1)} %collective-permute-done.12.refs_2_.refs_1_, bf16[4,64,512]{2,1,0:T(8,128)(2,1)S(1)} %collective-permute-done.13.refs_3_.refs_2_, ...), custom_call_target="tpu_custom_call" | custom-call | tf_op jit(solution)/shard_map/unpack/pallas_call | solution.py:222
  (41 shorter events, 2.8 us)
Async XLA Ops:
  0.0 1.6 %copy-start = (bf16[8,256,512]{2,1,0:T(8,128)(2,1)S(1)}, bf16[8,256,512]{2,1,0:T(8,128)(2,1)}, u32[]{:S(2)}) copy-start(bf16[8,256,512]{2,1,0:T(8,128)(2,1)} %ensemble_ref.3) | copy-start | bytes 6291460
  2.4 14.2 %collective-permute-start = (bf16[8,4,8,512]{3,2,1,0:T(8,128)(2,1)S(1)}, bf16[8,4,8,512]{3,2,1,0:T(8,128)(2,1)S(1)}, u32[]{:S(2)}, u32[]{:S(2)}) collective-permute-start(bf16[8,4,8,512]{3,2,1,0:T(8,128)(2,1)S(1)} %get-tuple-element.34), channel_id=1, source_target_pairs={{0,8},{8,0},{16,24},{24,16},{1,9},{9,1},{17,25},{25,17},{2,10},{10... | collective-permute-start | bytes 786440 | tf_op jit(solution)/shard_map/ppermute | solution.py:205
  5.5 21.4 %collective-permute-start.1 = (bf16[8,4,8,512]{3,2,1,0:T(8,128)(2,1)S(1)}, bf16[8,4,8,512]{3,2,1,0:T(8,128)(2,1)S(1)}, u32[]{:S(2)}, u32[]{:S(2)}) collective-permute-start(bf16[8,4,8,512]{3,2,1,0:T(8,128)(2,1)S(1)} %get-tuple-element.35), channel_id=1, source_target_pairs={{0,16},{8,24},{16,0},{24,8},{1,17},{9,25},{17,1},{25,9},{2,18},{10... | collective-permute-start | bytes 786440 | tf_op jit(solution)/shard_map/ppermute | solution.py:205
  8.1 26.2 %collective-permute-start.2 = (bf16[8,4,8,512]{3,2,1,0:T(8,128)(2,1)S(1)}, bf16[8,4,8,512]{3,2,1,0:T(8,128)(2,1)S(1)}, u32[]{:S(2)}, u32[]{:S(2)}) collective-permute-start(bf16[8,4,8,512]{3,2,1,0:T(8,128)(2,1)S(1)} %get-tuple-element.36), channel_id=1, source_target_pairs={{0,24},{8,16},{16,8},{24,0},{1,25},{9,17},{17,9},{25,1},{2,26},{10... | collective-permute-start | bytes 786440 | tf_op jit(solution)/shard_map/ppermute | solution.py:205
  8.1 5.8 %copy-start.1 = (s32[8,2048]{1,0:T(8,128)S(1)}, s32[8,2048]{1,0:T(8,128)}, u32[]{:S(2)}) copy-start(s32[8,2048]{1,0:T(8,128)} %site_ref.1) | copy-start | bytes 196612
  8.1 5.8 %copy-start.2 = (bf16[8,2048]{1,0:T(8,128)(2,1)S(1)}, bf16[8,2048]{1,0:T(8,128)(2,1)}, u32[]{:S(2)}) copy-start(bf16[8,2048]{1,0:T(8,128)(2,1)} %precision_ref.1) | copy-start | bytes 98308
  8.1 5.8 %copy-start.3 = (bf16[8,2048]{1,0:T(8,128)(2,1)S(1)}, bf16[8,2048]{1,0:T(8,128)(2,1)}, u32[]{:S(2)}) copy-start(bf16[8,2048]{1,0:T(8,128)(2,1)} %innovation_ref.1) | copy-start | bytes 98308
  8.1 5.8 %copy-start.4 = (s32[8]{0:T(128)S(1)}, s32[8]{0:T(128)}, u32[]{:S(2)}) copy-start(s32[8]{0:T(128)} %blocks_ref.1) | copy-start | bytes 100
  9.9 19.3 %all-to-all-start = ((bf16[8,4,4,8,512]{4,3,2,1,0:T(8,128)(2,1)}), bf16[8,4,4,8,512]{4,3,2,1,0:T(8,128)(2,1)S(1)}, u32[]{:S(2)}, u32[]{:S(2)}) async-start(bf16[8,4,4,8,512]{4,3,2,1,0:T(8,128)(2,1)} %pack.3.refs_0_), calls=%async_computation | async-start | bytes 2097152 | tf_op jit(solution)/shard_map/all_to_all | solution.py:202
  29.9 14.1 %collective-permute-start.3 = (bf16[2,64,512]{2,1,0:T(8,128)(2,1)S(1)}, bf16[2,64,512]{2,1,0:T(8,128)(2,1)S(1)}, u32[]{:S(2)}, u32[]{:S(2)}) collective-permute-start(bf16[2,64,512]{2,1,0:T(8,128)(2,1)S(1)} %get-tuple-element.38), channel_id=1, source_target_pairs={{0,8},{8,0},{16,24},{24,16},{1,9},{9,1},{17,25},{25,17},{2,10},{10... | collective-permute-start | bytes 393224 | tf_op jit(solution)/shard_map/ppermute | solution.py:205
  30.6 13.7 %collective-permute-start.4 = (bf16[2,64,512]{2,1,0:T(8,128)(2,1)}, bf16[2,64,512]{2,1,0:T(8,128)(2,1)S(1)}, u32[]{:S(2)}, u32[]{:S(2)}) collective-permute-start(bf16[2,64,512]{2,1,0:T(8,128)(2,1)} %get-tuple-element.39), channel_id=1, source_target_pairs={{0,16},{8,24},{16,0},{24,8},{1,17},{9,25},{17,1},{25,9},{2,18},{10... | collective-permute-start | bytes 393224 | tf_op jit(solution)/shard_map/ppermute | solution.py:205
  34.1 10.2 %collective-permute-start.5 = (bf16[2,64,512]{2,1,0:T(8,128)(2,1)S(1)}, bf16[2,64,512]{2,1,0:T(8,128)(2,1)}, u32[]{:S(2)}, u32[]{:S(2)}) collective-permute-start(bf16[2,64,512]{2,1,0:T(8,128)(2,1)S(1)} %get-tuple-element.40), channel_id=1, source_target_pairs={{0,24},{8,16},{16,8},{24,0},{1,25},{9,17},{17,9},{25,1},{2,26},{10... | collective-permute-start | bytes 393224 | tf_op jit(solution)/shard_map/ppermute | solution.py:205
  35.5 20.2 %all-to-all-start.1 = ((bf16[8,4,32,512]{3,2,1,0:T(8,128)(2,1)}), bf16[8,4,32,512]{3,2,1,0:T(8,128)(2,1)S(1)}, u32[]{:S(2)}, u32[]{:S(2)}) async-start(bf16[8,4,32,512]{3,2,1,0:T(8,128)(2,1)} %turn.6.refs_1_), calls=%async_computation.1 | async-start | bytes 2097152 | tf_op jit(solution)/shard_map/all_to_all | solution.py:202
  39.9 15.6 %collective-permute-start.6 = (bf16[2,64,512]{2,1,0:T(8,128)(2,1)S(1)}, bf16[2,64,512]{2,1,0:T(8,128)(2,1)S(1)}, u32[]{:S(2)}, u32[]{:S(2)}) collective-permute-start(bf16[2,64,512]{2,1,0:T(8,128)(2,1)S(1)} %get-tuple-element.43), channel_id=1, source_target_pairs={{0,8},{8,0},{16,24},{24,16},{1,9},{9,1},{17,25},{25,17},{2,10},{10... | collective-permute-start | bytes 393224 | tf_op jit(solution)/shard_map/ppermute | solution.py:205
  40.2 29.1 %collective-permute-start.7 = (bf16[2,64,512]{2,1,0:T(8,128)(2,1)}, bf16[2,64,512]{2,1,0:T(8,128)(2,1)S(1)}, u32[]{:S(2)}, u32[]{:S(2)}) collective-permute-start(bf16[2,64,512]{2,1,0:T(8,128)(2,1)} %get-tuple-element.44), channel_id=1, source_target_pairs={{0,16},{8,24},{16,0},{24,8},{1,17},{9,25},{17,1},{25,9},{2,18},{10... | collective-permute-start | bytes 393224 | tf_op jit(solution)/shard_map/ppermute | solution.py:205
  44.1 25.3 %collective-permute-start.8 = (bf16[2,64,512]{2,1,0:T(8,128)(2,1)S(1)}, bf16[2,64,512]{2,1,0:T(8,128)(2,1)S(1)}, u32[]{:S(2)}, u32[]{:S(2)}) collective-permute-start(bf16[2,64,512]{2,1,0:T(8,128)(2,1)S(1)} %get-tuple-element.45), channel_id=1, source_target_pairs={{0,24},{8,16},{16,8},{24,0},{1,25},{9,17},{17,9},{25,1},{2,26},{10... | collective-permute-start | bytes 393224 | tf_op jit(solution)/shard_map/ppermute | solution.py:205
  51.3 28.3 %collective-permute-start.9 = (bf16[8,2,8,512]{3,2,1,0:T(8,128)(2,1)}, bf16[8,2,8,512]{3,2,1,0:T(8,128)(2,1)S(1)}, u32[]{:S(2)}, u32[]{:S(2)}) collective-permute-start(bf16[8,2,8,512]{3,2,1,0:T(8,128)(2,1)} %get-tuple-element.47), channel_id=1, source_target_pairs={{0,8},{8,0},{16,24},{24,16},{1,9},{9,1},{17,25},{25,17},{2,10},{10... | collective-permute-start | bytes 393224 | tf_op jit(solution)/shard_map/ppermute | solution.py:205
  51.6 28.2 %collective-permute-start.10 = (bf16[8,2,8,512]{3,2,1,0:T(8,128)(2,1)}, bf16[8,2,8,512]{3,2,1,0:T(8,128)(2,1)S(1)}, u32[]{:S(2)}, u32[]{:S(2)}) collective-permute-start(bf16[8,2,8,512]{3,2,1,0:T(8,128)(2,1)} %get-tuple-element.48), channel_id=1, source_target_pairs={{0,16},{8,24},{16,0},{24,8},{1,17},{9,25},{17,1},{25,9},{2,18},{10... | collective-permute-start | bytes 393224 | tf_op jit(solution)/shard_map/ppermute | solution.py:205
  55.4 24.4 %collective-permute-start.11 = (bf16[8,2,8,512]{3,2,1,0:T(8,128)(2,1)S(1)}, bf16[8,2,8,512]{3,2,1,0:T(8,128)(2,1)S(1)}, u32[]{:S(2)}, u32[]{:S(2)}) collective-permute-start(bf16[8,2,8,512]{3,2,1,0:T(8,128)(2,1)S(1)} %get-tuple-element.49), channel_id=1, source_target_pairs={{0,24},{8,16},{16,8},{24,0},{1,25},{9,17},{17,9},{25,1},{2,26},{10... | collective-permute-start | bytes 393224 | tf_op jit(solution)/shard_map/ppermute | solution.py:205
  65.4 19.4 %all-to-all-start.2 = ((bf16[8,4,4,8,512]{4,3,2,1,0:T(8,128)(2,1)}), bf16[8,4,4,8,512]{4,3,2,1,0:T(8,128)(2,1)S(1)}, u32[]{:S(2)}, u32[]{:S(2)}) async-start(bf16[8,4,4,8,512]{4,3,2,1,0:T(8,128)(2,1)} %analyse.4.refs_4_), calls=%async_computation.2 | async-start | bytes 2097152 | tf_op jit(solution)/shard_map/all_to_all | solution.py:202
  75.5 13.7 %collective-permute-start.15 = (bf16[8,2,8,512]{3,2,1,0:T(8,128)(2,1)S(1)}, bf16[8,2,8,512]{3,2,1,0:T(8,128)(2,1)S(1)}, u32[]{:S(2)}, u32[]{:S(2)}) collective-permute-start(bf16[8,2,8,512]{3,2,1,0:T(8,128)(2,1)S(1)} %get-tuple-element.54), channel_id=1, source_target_pairs={{0,8},{8,0},{16,24},{24,16},{1,9},{9,1},{17,25},{25,17},{2,10},{10... | collective-permute-start | bytes 393224 | tf_op jit(solution)/shard_map/ppermute | solution.py:205
  75.8 14.2 %collective-permute-start.16 = (bf16[8,2,8,512]{3,2,1,0:T(8,128)(2,1)}, bf16[8,2,8,512]{3,2,1,0:T(8,128)(2,1)}, u32[]{:S(2)}, u32[]{:S(2)}) collective-permute-start(bf16[8,2,8,512]{3,2,1,0:T(8,128)(2,1)} %get-tuple-element.55), channel_id=1, source_target_pairs={{0,16},{8,24},{16,0},{24,8},{1,17},{9,25},{17,1},{25,9},{2,18},{10... | collective-permute-start | bytes 393224 | tf_op jit(solution)/shard_map/ppermute | solution.py:205
  79.6 10.4 %collective-permute-start.17 = (bf16[8,2,8,512]{3,2,1,0:T(8,128)(2,1)}, bf16[8,2,8,512]{3,2,1,0:T(8,128)(2,1)}, u32[]{:S(2)}, u32[]{:S(2)}) collective-permute-start(bf16[8,2,8,512]{3,2,1,0:T(8,128)(2,1)} %get-tuple-element.56), channel_id=1, source_target_pairs={{0,24},{8,16},{16,8},{24,0},{1,25},{9,17},{17,9},{25,1},{2,26},{10... | collective-permute-start | bytes 393224 | tf_op jit(solution)/shard_map/ppermute | solution.py:205
  84.9 12.2 %collective-permute-start.12 = (bf16[4,64,512]{2,1,0:T(8,128)(2,1)S(1)}, bf16[4,64,512]{2,1,0:T(8,128)(2,1)S(1)}, u32[]{:S(2)}, u32[]{:S(2)}) collective-permute-start(bf16[4,64,512]{2,1,0:T(8,128)(2,1)S(1)} %get-tuple-element.51), channel_id=1, source_target_pairs={{0,8},{8,0},{16,24},{24,16},{1,9},{9,1},{17,25},{25,17},{2,10},{10... | collective-permute-start | bytes 786440 | tf_op jit(solution)/shard_map/ppermute | solution.py:205
  85.3 24.1 %collective-permute-start.13 = (bf16[4,64,512]{2,1,0:T(8,128)(2,1)S(1)}, bf16[4,64,512]{2,1,0:T(8,128)(2,1)S(1)}, u32[]{:S(2)}, u32[]{:S(2)}) collective-permute-start(bf16[4,64,512]{2,1,0:T(8,128)(2,1)S(1)} %get-tuple-element.52), channel_id=1, source_target_pairs={{0,16},{8,24},{16,0},{24,8},{1,17},{9,25},{17,1},{25,9},{2,18},{10... | collective-permute-start | bytes 786440 | tf_op jit(solution)/shard_map/ppermute | solution.py:205
  89.1 0.7 copy-start.5
  89.8 19.7 %collective-permute-start.14 = (bf16[4,64,512]{2,1,0:T(8,128)(2,1)S(1)}, bf16[4,64,512]{2,1,0:T(8,128)(2,1)S(1)}, u32[]{:S(2)}, u32[]{:S(2)}) collective-permute-start(bf16[4,64,512]{2,1,0:T(8,128)(2,1)S(1)} %get-tuple-element.53), channel_id=1, source_target_pairs={{0,24},{8,16},{16,8},{24,0},{1,25},{9,17},{17,9},{25,1},{2,26},{10... | collective-permute-start | bytes 786440 | tf_op jit(solution)/shard_map/ppermute | solution.py:205
  90.0 0.9 copy-start.6
  93.0 19.5 %all-to-all-start.3 = ((bf16[8,4,32,512]{3,2,1,0:T(8,128)(2,1)}), bf16[8,4,32,512]{3,2,1,0:T(8,128)(2,1)S(1)}, u32[]{:S(2)}, u32[]{:S(2)}) async-start(bf16[8,4,32,512]{3,2,1,0:T(8,128)(2,1)} %turn.9.refs_0_), calls=%async_computation.3 | async-start | bytes 2097152 | tf_op jit(solution)/shard_map/all_to_all | solution.py:202
